TPU v7x, 128 devices: a whole 4x4x4 slice. The times are simulated.
128 devices in a mesh: dp: 8 (over x, y_hi), seq: 16 (over z, y_lo, core).
Axes of the slice: x: 4, y: 4 (y_hi: 2, y_lo: 2; y = y_hi * 2 + y_lo), z: 4, core: 2. Of those that a mesh axis runs over, the one named last changes fastest.
Arguments:
- tokens: bfloat16 [8, 8192, 2048], P('dp', 'seq'), may hold values from -6 to 6
- w_query: bfloat16 [2048, 1024], replicated, may hold values from -0.125 to 0.125
- keys: bfloat16 [8, 8192, 1024], P('dp', 'seq'), may hold values from -0.5 to 0.5
- values: bfloat16 [8, 8192, 1024], P('dp', 'seq'), may hold values from -6 to 6
- log_decay: float32 [8, 8, 8192], P('dp', None, 'seq'), may hold values from -0.76640625 to 0, as said below
- regular: float32 [8], replicated, may hold values from 1 to 8
- grad_out: bfloat16 [8, 8192, 1024], P('dp', 'seq'), may hold values from -0.0234375 to 0.0234375
Outputs:
- mixed: bfloat16 [8, 8192, 1024], P('dp', 'seq')
- query_grad: float32 [1024, 2048], P('dp', 'seq')
Inputs may be any that keep to these rules, and one draw needn't show every extreme that they name: `log_decay`: a head's decay varies from position to position.
All inputs are finite; a program needn't handle non-finite values.
Results may differ from a plain program's by a relative error of at most 0.0049.
Values sent between devices are 32-bit elements; how exact they have to be, the bound alone decides.
A program may use at most 64 MiB of HBM per device.

v0:
```python
import jax
import jax.numpy as jnp
from jax import lax
from jax.sharding import PartitionSpec as P

ITERS = 4


exact_mode = lax.Precision.HIGHEST
split_mode = lax.Precision.HIGH


def passed_along(value, axis, steps):
    count = lax.axis_size(axis)
    initial, last = (max(0, -steps), min(count, count - steps))
    return lax.ppermute(value, axis, [(source, source + steps) for source in range(initial, last)])


def product(left, right):
    return jnp.dot(left, right, precision=exact_mode)


def mixed_product(left, right):
    return jnp.dot(left, right, precision=split_mode, preferred_element_type=jnp.float32)


def plain_product(left, right):
    return jnp.dot(left, right, preferred_element_type=jnp.float32)


def decay_table(cumulative):
    token_positions = jnp.arange(cumulative.shape[0])
    lower_mask = token_positions[:, None] >= token_positions[None, :]
    spread = cumulative[:, None] - cumulative[None, :]
    return jnp.where(lower_mask, jnp.exp(jnp.where(lower_mask, spread, 0.0)), 0.0)


def chebyshev(right_side, apply_fn, center, half_span):
    solution = jnp.zeros_like(right_side)
    residual = right_side
    search = right_side
    step_size = 1.0 / center
    for index_step in range(ITERS):
        if index_step > 0:
            factor = 0.5 if index_step == 1 else 0.25
            momentum = factor * (half_span * step_size) ** 2
            step_size = 1.0 / (center - momentum / step_size)
            search = residual + momentum * search
        solution = solution + step_size * search
        if index_step + 1 < ITERS:
            residual = residual - step_size * apply_fn(search)
    return solution


def solve_group(queries, key_rows, value_rows, grad_half, cumulative, ridge, gram_state, memory):
    weights = decay_table(cumulative)
    scale = jnp.exp(cumulative)[:, None]
    key_square = jnp.sum(jnp.square(key_rows.astype(jnp.float32)), axis=1)
    trace_rows = scale[:, 0] * jnp.trace(gram_state) + product(weights, key_square)
    half_span = 0.5 * trace_rows[:, None]
    center = ridge + half_span
    right_query = queries.astype(jnp.float32)
    grad_rows = grad_half.astype(jnp.float32)

    def apply_fn(search):
        return (
            ridge * search
            + scale * product(search, gram_state)
            + mixed_product(weights * mixed_product(search, key_rows.T), key_rows)
        )

    solved = chebyshev(right_query, apply_fn, center, half_span)
    output = scale * product(solved, memory.T) + mixed_product(
        weights * mixed_product(solved, key_rows.T), value_rows
    )
    pulled = scale * product(grad_rows, memory) + mixed_product(
        weights * plain_product(grad_half, value_rows.T), key_rows
    )
    query_rows = chebyshev(pulled, apply_fn, center, half_span)
    return (output, query_rows)


def local_states(key_rows, value_rows, cumulative):
    tail_weight = jnp.exp(cumulative[-1] - cumulative)[:, None]
    return (
        mixed_product((key_rows * tail_weight).T, key_rows),
        mixed_product((value_rows * tail_weight).T, key_rows),
    )


def solve_item(item_set):
    return solve_group(*item_set)


def per_device(tokens, w_query, keys, values, log_decay, regular, grad_out):
    seqs, rows, width = tokens.shape
    heads = log_decay.shape[1]
    columns = keys.shape[2]
    head_dim = columns // heads
    flat_tokens = tokens.reshape(seqs * rows, width)
    queries = jnp.dot(flat_tokens, w_query, preferred_element_type=jnp.float32).astype(jnp.bfloat16)
    queries = lax.optimization_barrier(queries)

    def to_heads(array):
        return array.reshape(seqs, rows, heads, head_dim).transpose(0, 2, 1, 3)

    key_heads = to_heads(keys)
    value_heads = to_heads(values)
    cumulative = jnp.cumsum(log_decay, axis=2)
    gram_local, memory_local = jax.vmap(jax.vmap(local_states))(key_heads, value_heads, cumulative)
    last_decay = jnp.exp(cumulative[:, :, -1])
    widened = last_decay[:, :, None, None]

    def hand_over(index_step, carried):
        incoming, outgoing = carried
        incoming = passed_along((outgoing[0], outgoing[1]), "seq", 1)
        outgoing = (widened * incoming[0] + gram_local, widened * incoming[1] + memory_local)
        return (incoming, outgoing)

    empty = (jnp.zeros_like(gram_local), jnp.zeros_like(memory_local))
    incoming, outgoing = lax.fori_loop(
        0, lax.axis_size("seq") - 1, hand_over, (empty, (gram_local, memory_local))
    )
    gram_start, memory_start = incoming
    ridge = regular[None, :].reshape(seqs * heads)
    items = (
        to_heads(queries).reshape(seqs * heads, rows, head_dim),
        key_heads.reshape(seqs * heads, rows, head_dim),
        value_heads.reshape(seqs * heads, rows, head_dim),
        to_heads(grad_out).reshape(seqs * heads, rows, head_dim),
        cumulative.reshape(seqs * heads, rows),
        ridge,
        gram_start.reshape(seqs * heads, head_dim, head_dim),
        memory_start.reshape(seqs * heads, head_dim, head_dim),
    )
    outputs, query_rows = lax.map(solve_item, items)

    def from_heads(array):
        return (
            array.reshape(seqs, heads, rows, head_dim)
            .transpose(0, 2, 1, 3)
            .reshape(seqs, rows, columns)
        )

    mixed = from_heads(outputs).astype(jnp.bfloat16)
    grad_flat = from_heads(query_rows).astype(jnp.bfloat16).reshape(seqs * rows, columns)
    terms = lax.dot_general(
        grad_flat, flat_tokens, (((0,), (0,)), ((), ())), preferred_element_type=jnp.float32
    )
    partial_sum = lax.psum_scatter(terms, "seq", scatter_dimension=1, tiled=True)
    query_grad = lax.psum_scatter(partial_sum, "dp", scatter_dimension=0, tiled=True)
    return (mixed, query_grad)


def solution(mesh):
    in_specs = (
        P("dp", "seq", None),
        P(),
        P("dp", "seq", None),
        P("dp", "seq", None),
        P("dp", None, "seq"),
        P(),
        P("dp", "seq", None),
    )
    out_specs = (P("dp", "seq", None), P("dp", "seq"))
    return jax.shard_map(
        per_device, mesh=mesh, in_specs=in_specs, out_specs=out_specs, check_vma=False
    )
```

profile of v0, /device:TPU:1, one launch (start us, length us, event | category | flops | bytes accessed | tf_op | source)
XLA Modules:
  0.0 726.8 jit_solution(7861904356463987452)
XLA Ops:
  21.2 4.5 fusion.140
  29.4 290.4 %while.28 = (s32[]{:T(128)}, f32[1,8,128,128]{3,2,1,0:T(8,128)}, f32[1,8,128,128]{3,2,1,0:T(8,128)}, f32[1,8,128,128]{3,2,1,0:T(8,128)S(1)}, f32[1,8,128,128]{3,...) while((s32[]{:T(128)}, f32[1,8,128,128]{3,2,1,0:T(8,128)}, ...), condition=%wide.region_3.4_spmd, body=%wide.region_2.3_spmd.sunk | while | flops 524290 | bytes 9437417 | solution.py:121
  29.5 4.7 collective-permute-start.1
  36.1 4.5 collective-permute-done.1
  40.6 5.5 collective-permute-done
  46.1 2.5 multiply_add_fusion.20
  48.6 4.4 collective-permute-start.1
  55.0 4.5 collective-permute-done.1
  59.5 5.5 collective-permute-done
  65.0 2.5 multiply_add_fusion.20
  67.5 4.4 collective-permute-start.1
  74.1 4.2 collective-permute-done.1
  78.3 5.5 collective-permute-done
  83.8 2.5 multiply_add_fusion.20
  86.4 4.4 collective-permute-start.1
  90.7 3.1 collective-permute-start
  93.9 3.3 collective-permute-done.1
  97.2 5.5 collective-permute-done
  102.7 2.5 multiply_add_fusion.20
  105.2 4.4 collective-permute-start.1
  109.6 4.0 collective-permute-start
  116.0 5.5 collective-permute-done
  121.5 2.5 multiply_add_fusion.20
  124.1 4.4 collective-permute-start.1
  128.5 4.9 collective-permute-start
  134.9 5.5 collective-permute-done
  140.4 2.5 multiply_add_fusion.20
  142.9 4.4 collective-permute-start.1
  147.3 5.8 collective-permute-start
  153.7 5.5 collective-permute-done
  159.3 2.5 multiply_add_fusion.20
  161.8 4.4 collective-permute-start.1
  166.2 6.7 collective-permute-start
  172.9 6.1 collective-permute-done
  179.0 2.5 multiply_add_fusion.20
  181.6 4.4 collective-permute-start.1
  185.9 6.7 collective-permute-start
  192.7 6.1 collective-permute-done
  198.8 2.5 multiply_add_fusion.20
  201.3 4.4 collective-permute-start.1
  205.7 6.7 collective-permute-start
  212.4 6.1 collective-permute-done
  218.5 2.5 multiply_add_fusion.20
  221.1 4.4 collective-permute-start.1
  225.5 6.7 collective-permute-start
  232.2 6.1 collective-permute-done
  238.3 2.5 multiply_add_fusion.20
  240.8 4.4 collective-permute-start.1
  245.2 6.7 collective-permute-start
  251.9 6.1 collective-permute-done
  258.0 2.5 multiply_add_fusion.20
  260.6 4.4 collective-permute-start.1
  265.0 6.7 collective-permute-start
  271.7 6.1 collective-permute-done
  280.3 4.4 collective-permute-start.1
  284.7 6.7 collective-permute-start
  291.5 6.1 collective-permute-done
  300.1 4.4 collective-permute-start.1
  304.5 6.7 collective-permute-start
  311.2 6.1 collective-permute-done
  319.8 214.4 %while.29 = (s32[]{:T(128)}, bf16[8,512,128]{2,1,0:T(8,128)(2,1)}, bf16[8,512,128]{1,2,0:T(8,128)(2,1)}, f32[8,512]{1,0:T(8,128)S(1)}, f32[8]{0:T(128)S(1)}, /*i...) while((s32[]{:T(128)}, bf16[8,512,128]{2,1,0:T(8,128)(2,1)}, ...), condition=%wide.region_7.8_spmd, body=%wide.region_4.7_spmd.sunk | while | flops 3779724288 | bytes 42295060 | solution.py:136
  534.3 6.8 fusion.128
  541.1 105.5 %reduce-scatter.3.cloned.1.call-done = f32[1024,128]{1,0:T(8,128)} async-done(((f32[1024,2048]{1,0:T(8,128)}), f32[1024,128]{1,0:T(8,128)}) %reduce-scatter.3.cloned.1.call-update) | async-done | bytes 524304 | tf_op jit(solution)/shard_map/reduce_scatter | solution.py:150
  647.8 72.1 %reduce-scatter.5.cloned.1.call-done = f32[128,128]{1,0:T(8,128)} async-done(((f32[1024,128]{1,0:T(8,128)}), f32[128,128]{1,0:T(8,128)}) %reduce-scatter.5.cloned.1.call-update) | async-done | bytes 65552 | tf_op jit(solution)/shard_map/reduce_scatter | solution.py:151
  (395 shorter events, 249.7 us)
Async XLA Ops:
  7.2 14.0 %copy-start = (bf16[1,512,2048]{2,1,0:T(8,128)(2,1)S(1)}, bf16[1,512,2048]{2,1,0:T(8,128)(2,1)}, u32[]{:S(2)}) copy-start(bf16[1,512,2048]{2,1,0:T(8,128)(2,1)} %param.11) | copy-start | bytes 6291460
  7.2 639.5 %reduce-scatter.3.cloned.1.call-start = ((), (), s32[]{:S(2)}) async-start(), calls=%async_computation.2 | async-start | bytes 8912896 | tf_op jit(solution)/shard_map/reduce_scatter | solution.py:150
  14.8 4.8 copy-start.3
  26.0 3.5 copy-start.4
  29.4 290.4 %copy-start.8 = (f32[8]{0:T(128)S(1)}, f32[8]{0:T(128)}, u32[]{:S(2)}) copy-start(f32[8]{0:T(128)} %param.16) | copy-start | bytes 100
  29.5 11.1 %collective-permute-start.1 = (f32[1,8,128,128]{3,2,1,0:T(8,128)}, f32[1,8,128,128]{3,2,1,0:T(8,128)}, u32[]{:S(2)}, u32[]{:S(2)}) collective-permute-start(f32[1,8,128,128]{3,2,1,0:T(8,128)} %get-tuple-element.330), channel_id=1, source_target_pairs={{0,1},{1,2},{2,3},{3,4},{4,5},{5,6},{6,7},{7,8},{8,9},{9,10},{10,1... | collective-permute-start | bytes 1572872 | tf_op jit(solution)/shard_map/while/body/eval_jaxpr/ppermute | solution.py:16
  34.2 11.9 %collective-permute-start = (f32[1,8,128,128]{3,2,1,0:T(8,128)S(1)}, f32[1,8,128,128]{3,2,1,0:T(8,128)S(1)}, u32[]{:S(2)}, u32[]{:S(2)}) collective-permute-start(f32[1,8,128,128]{3,2,1,0:T(8,128)S(1)} %get-tuple-element.329), channel_id=1, source_target_pairs={{0,1},{1,2},{2,3},{3,4},{4,5},{5,6},{6,7},{7,8},{8,9},{9,10},{10,1... | collective-permute-start | bytes 1572872 | tf_op jit(solution)/shard_map/while/body/eval_jaxpr/ppermute | solution.py:16
  46.1 2.5 copy-start.1
  48.6 10.8 %collective-permute-start.1 = (f32[1,8,128,128]{3,2,1,0:T(8,128)}, f32[1,8,128,128]{3,2,1,0:T(8,128)}, u32[]{:S(2)}, u32[]{:S(2)}) collective-permute-start(f32[1,8,128,128]{3,2,1,0:T(8,128)} %get-tuple-element.330), channel_id=1, source_target_pairs={{0,1},{1,2},{2,3},{3,4},{4,5},{5,6},{6,7},{7,8},{8,9},{9,10},{10,1... | collective-permute-start | bytes 1572872 | tf_op jit(solution)/shard_map/while/body/eval_jaxpr/ppermute | solution.py:16
  53.0 11.9 %collective-permute-start = (f32[1,8,128,128]{3,2,1,0:T(8,128)S(1)}, f32[1,8,128,128]{3,2,1,0:T(8,128)S(1)}, u32[]{:S(2)}, u32[]{:S(2)}) collective-permute-start(f32[1,8,128,128]{3,2,1,0:T(8,128)S(1)} %get-tuple-element.329), channel_id=1, source_target_pairs={{0,1},{1,2},{2,3},{3,4},{4,5},{5,6},{6,7},{7,8},{8,9},{9,10},{10,1... | collective-permute-start | bytes 1572872 | tf_op jit(solution)/shard_map/while/body/eval_jaxpr/ppermute | solution.py:16
  65.0 2.5 copy-start.1
  67.5 10.8 %collective-permute-start.1 = (f32[1,8,128,128]{3,2,1,0:T(8,128)}, f32[1,8,128,128]{3,2,1,0:T(8,128)}, u32[]{:S(2)}, u32[]{:S(2)}) collective-permute-start(f32[1,8,128,128]{3,2,1,0:T(8,128)} %get-tuple-element.330), channel_id=1, source_target_pairs={{0,1},{1,2},{2,3},{3,4},{4,5},{5,6},{6,7},{7,8},{8,9},{9,10},{10,1... | collective-permute-start | bytes 1572872 | tf_op jit(solution)/shard_map/while/body/eval_jaxpr/ppermute | solution.py:16
  71.9 11.9 %collective-permute-start = (f32[1,8,128,128]{3,2,1,0:T(8,128)S(1)}, f32[1,8,128,128]{3,2,1,0:T(8,128)S(1)}, u32[]{:S(2)}, u32[]{:S(2)}) collective-permute-start(f32[1,8,128,128]{3,2,1,0:T(8,128)S(1)} %get-tuple-element.329), channel_id=1, source_target_pairs={{0,1},{1,2},{2,3},{3,4},{4,5},{5,6},{6,7},{7,8},{8,9},{9,10},{10,1... | collective-permute-start | bytes 1572872 | tf_op jit(solution)/shard_map/while/body/eval_jaxpr/ppermute | solution.py:16
  83.8 2.5 copy-start.1
  86.4 10.8 %collective-permute-start.1 = (f32[1,8,128,128]{3,2,1,0:T(8,128)}, f32[1,8,128,128]{3,2,1,0:T(8,128)}, u32[]{:S(2)}, u32[]{:S(2)}) collective-permute-start(f32[1,8,128,128]{3,2,1,0:T(8,128)} %get-tuple-element.330), channel_id=1, source_target_pairs={{0,1},{1,2},{2,3},{3,4},{4,5},{5,6},{6,7},{7,8},{8,9},{9,10},{10,1... | collective-permute-start | bytes 1572872 | tf_op jit(solution)/shard_map/while/body/eval_jaxpr/ppermute | solution.py:16
  90.7 11.9 %collective-permute-start = (f32[1,8,128,128]{3,2,1,0:T(8,128)S(1)}, f32[1,8,128,128]{3,2,1,0:T(8,128)S(1)}, u32[]{:S(2)}, u32[]{:S(2)}) collective-permute-start(f32[1,8,128,128]{3,2,1,0:T(8,128)S(1)} %get-tuple-element.329), channel_id=1, source_target_pairs={{0,1},{1,2},{2,3},{3,4},{4,5},{5,6},{6,7},{7,8},{8,9},{9,10},{10,1... | collective-permute-start | bytes 1572872 | tf_op jit(solution)/shard_map/while/body/eval_jaxpr/ppermute | solution.py:16
  102.7 2.5 copy-start.1
  105.2 10.8 %collective-permute-start.1 = (f32[1,8,128,128]{3,2,1,0:T(8,128)}, f32[1,8,128,128]{3,2,1,0:T(8,128)}, u32[]{:S(2)}, u32[]{:S(2)}) collective-permute-start(f32[1,8,128,128]{3,2,1,0:T(8,128)} %get-tuple-element.330), channel_id=1, source_target_pairs={{0,1},{1,2},{2,3},{3,4},{4,5},{5,6},{6,7},{7,8},{8,9},{9,10},{10,1... | collective-permute-start | bytes 1572872 | tf_op jit(solution)/shard_map/while/body/eval_jaxpr/ppermute | solution.py:16
  109.6 11.9 %collective-permute-start = (f32[1,8,128,128]{3,2,1,0:T(8,128)S(1)}, f32[1,8,128,128]{3,2,1,0:T(8,128)S(1)}, u32[]{:S(2)}, u32[]{:S(2)}) collective-permute-start(f32[1,8,128,128]{3,2,1,0:T(8,128)S(1)} %get-tuple-element.329), channel_id=1, source_target_pairs={{0,1},{1,2},{2,3},{3,4},{4,5},{5,6},{6,7},{7,8},{8,9},{9,10},{10,1... | collective-permute-start | bytes 1572872 | tf_op jit(solution)/shard_map/while/body/eval_jaxpr/ppermute | solution.py:16
  121.5 2.5 copy-start.1
  124.1 10.8 %collective-permute-start.1 = (f32[1,8,128,128]{3,2,1,0:T(8,128)}, f32[1,8,128,128]{3,2,1,0:T(8,128)}, u32[]{:S(2)}, u32[]{:S(2)}) collective-permute-start(f32[1,8,128,128]{3,2,1,0:T(8,128)} %get-tuple-element.330), channel_id=1, source_target_pairs={{0,1},{1,2},{2,3},{3,4},{4,5},{5,6},{6,7},{7,8},{8,9},{9,10},{10,1... | collective-permute-start | bytes 1572872 | tf_op jit(solution)/shard_map/while/body/eval_jaxpr/ppermute | solution.py:16
  128.5 11.9 %collective-permute-start = (f32[1,8,128,128]{3,2,1,0:T(8,128)S(1)}, f32[1,8,128,128]{3,2,1,0:T(8,128)S(1)}, u32[]{:S(2)}, u32[]{:S(2)}) collective-permute-start(f32[1,8,128,128]{3,2,1,0:T(8,128)S(1)} %get-tuple-element.329), channel_id=1, source_target_pairs={{0,1},{1,2},{2,3},{3,4},{4,5},{5,6},{6,7},{7,8},{8,9},{9,10},{10,1... | collective-permute-start | bytes 1572872 | tf_op jit(solution)/shard_map/while/body/eval_jaxpr/ppermute | solution.py:16
  140.4 2.5 copy-start.1
  142.9 10.8 %collective-permute-start.1 = (f32[1,8,128,128]{3,2,1,0:T(8,128)}, f32[1,8,128,128]{3,2,1,0:T(8,128)}, u32[]{:S(2)}, u32[]{:S(2)}) collective-permute-start(f32[1,8,128,128]{3,2,1,0:T(8,128)} %get-tuple-element.330), channel_id=1, source_target_pairs={{0,1},{1,2},{2,3},{3,4},{4,5},{5,6},{6,7},{7,8},{8,9},{9,10},{10,1... | collective-permute-start | bytes 1572872 | tf_op jit(solution)/shard_map/while/body/eval_jaxpr/ppermute | solution.py:16
  147.3 12.0 %collective-permute-start = (f32[1,8,128,128]{3,2,1,0:T(8,128)S(1)}, f32[1,8,128,128]{3,2,1,0:T(8,128)S(1)}, u32[]{:S(2)}, u32[]{:S(2)}) collective-permute-start(f32[1,8,128,128]{3,2,1,0:T(8,128)S(1)} %get-tuple-element.329), channel_id=1, source_target_pairs={{0,1},{1,2},{2,3},{3,4},{4,5},{5,6},{6,7},{7,8},{8,9},{9,10},{10,1... | collective-permute-start | bytes 1572872 | tf_op jit(solution)/shard_map/while/body/eval_jaxpr/ppermute | solution.py:16
  159.3 2.5 copy-start.1
  161.8 11.1 %collective-permute-start.1 = (f32[1,8,128,128]{3,2,1,0:T(8,128)}, f32[1,8,128,128]{3,2,1,0:T(8,128)}, u32[]{:S(2)}, u32[]{:S(2)}) collective-permute-start(f32[1,8,128,128]{3,2,1,0:T(8,128)} %get-tuple-element.330), channel_id=1, source_target_pairs={{0,1},{1,2},{2,3},{3,4},{4,5},{5,6},{6,7},{7,8},{8,9},{9,10},{10,1... | collective-permute-start | bytes 1572872 | tf_op jit(solution)/shard_map/while/body/eval_jaxpr/ppermute | solution.py:16
  166.2 12.8 %collective-permute-start = (f32[1,8,128,128]{3,2,1,0:T(8,128)S(1)}, f32[1,8,128,128]{3,2,1,0:T(8,128)S(1)}, u32[]{:S(2)}, u32[]{:S(2)}) collective-permute-start(f32[1,8,128,128]{3,2,1,0:T(8,128)S(1)} %get-tuple-element.329), channel_id=1, source_target_pairs={{0,1},{1,2},{2,3},{3,4},{4,5},{5,6},{6,7},{7,8},{8,9},{9,10},{10,1... | collective-permute-start | bytes 1572872 | tf_op jit(solution)/shard_map/while/body/eval_jaxpr/ppermute | solution.py:16
  179.0 2.5 copy-start.1
  181.6 11.1 %collective-permute-start.1 = (f32[1,8,128,128]{3,2,1,0:T(8,128)}, f32[1,8,128,128]{3,2,1,0:T(8,128)}, u32[]{:S(2)}, u32[]{:S(2)}) collective-permute-start(f32[1,8,128,128]{3,2,1,0:T(8,128)} %get-tuple-element.330), channel_id=1, source_target_pairs={{0,1},{1,2},{2,3},{3,4},{4,5},{5,6},{6,7},{7,8},{8,9},{9,10},{10,1... | collective-permute-start | bytes 1572872 | tf_op jit(solution)/shard_map/while/body/eval_jaxpr/ppermute | solution.py:16
  185.9 12.8 %collective-permute-start = (f32[1,8,128,128]{3,2,1,0:T(8,128)S(1)}, f32[1,8,128,128]{3,2,1,0:T(8,128)S(1)}, u32[]{:S(2)}, u32[]{:S(2)}) collective-permute-start(f32[1,8,128,128]{3,2,1,0:T(8,128)S(1)} %get-tuple-element.329), channel_id=1, source_target_pairs={{0,1},{1,2},{2,3},{3,4},{4,5},{5,6},{6,7},{7,8},{8,9},{9,10},{10,1... | collective-permute-start | bytes 1572872 | tf_op jit(solution)/shard_map/while/body/eval_jaxpr/ppermute | solution.py:16
  198.8 2.5 copy-start.1
  201.3 11.1 %collective-permute-start.1 = (f32[1,8,128,128]{3,2,1,0:T(8,128)}, f32[1,8,128,128]{3,2,1,0:T(8,128)}, u32[]{:S(2)}, u32[]{:S(2)}) collective-permute-start(f32[1,8,128,128]{3,2,1,0:T(8,128)} %get-tuple-element.330), channel_id=1, source_target_pairs={{0,1},{1,2},{2,3},{3,4},{4,5},{5,6},{6,7},{7,8},{8,9},{9,10},{10,1... | collective-permute-start | bytes 1572872 | tf_op jit(solution)/shard_map/while/body/eval_jaxpr/ppermute | solution.py:16
  205.7 12.8 %collective-permute-start = (f32[1,8,128,128]{3,2,1,0:T(8,128)S(1)}, f32[1,8,128,128]{3,2,1,0:T(8,128)S(1)}, u32[]{:S(2)}, u32[]{:S(2)}) collective-permute-start(f32[1,8,128,128]{3,2,1,0:T(8,128)S(1)} %get-tuple-element.329), channel_id=1, source_target_pairs={{0,1},{1,2},{2,3},{3,4},{4,5},{5,6},{6,7},{7,8},{8,9},{9,10},{10,1... | collective-permute-start | bytes 1572872 | tf_op jit(solution)/shard_map/while/body/eval_jaxpr/ppermute | solution.py:16
  218.5 2.5 copy-start.1
  221.1 11.1 %collective-permute-start.1 = (f32[1,8,128,128]{3,2,1,0:T(8,128)}, f32[1,8,128,128]{3,2,1,0:T(8,128)}, u32[]{:S(2)}, u32[]{:S(2)}) collective-permute-start(f32[1,8,128,128]{3,2,1,0:T(8,128)} %get-tuple-element.330), channel_id=1, source_target_pairs={{0,1},{1,2},{2,3},{3,4},{4,5},{5,6},{6,7},{7,8},{8,9},{9,10},{10,1... | collective-permute-start | bytes 1572872 | tf_op jit(solution)/shard_map/while/body/eval_jaxpr/ppermute | solution.py:16
  225.5 12.8 %collective-permute-start = (f32[1,8,128,128]{3,2,1,0:T(8,128)S(1)}, f32[1,8,128,128]{3,2,1,0:T(8,128)S(1)}, u32[]{:S(2)}, u32[]{:S(2)}) collective-permute-start(f32[1,8,128,128]{3,2,1,0:T(8,128)S(1)} %get-tuple-element.329), channel_id=1, source_target_pairs={{0,1},{1,2},{2,3},{3,4},{4,5},{5,6},{6,7},{7,8},{8,9},{9,10},{10,1... | collective-permute-start | bytes 1572872 | tf_op jit(solution)/shard_map/while/body/eval_jaxpr/ppermute | solution.py:16
  240.8 11.1 %collective-permute-start.1 = (f32[1,8,128,128]{3,2,1,0:T(8,128)}, f32[1,8,128,128]{3,2,1,0:T(8,128)}, u32[]{:S(2)}, u32[]{:S(2)}) collective-permute-start(f32[1,8,128,128]{3,2,1,0:T(8,128)} %get-tuple-element.330), channel_id=1, source_target_pairs={{0,1},{1,2},{2,3},{3,4},{4,5},{5,6},{6,7},{7,8},{8,9},{9,10},{10,1... | collective-permute-start | bytes 1572872 | tf_op jit(solution)/shard_map/while/body/eval_jaxpr/ppermute | solution.py:16
  245.2 12.8 %collective-permute-start = (f32[1,8,128,128]{3,2,1,0:T(8,128)S(1)}, f32[1,8,128,128]{3,2,1,0:T(8,128)S(1)}, u32[]{:S(2)}, u32[]{:S(2)}) collective-permute-start(f32[1,8,128,128]{3,2,1,0:T(8,128)S(1)} %get-tuple-element.329), channel_id=1, source_target_pairs={{0,1},{1,2},{2,3},{3,4},{4,5},{5,6},{6,7},{7,8},{8,9},{9,10},{10,1... | collective-permute-start | bytes 1572872 | tf_op jit(solution)/shard_map/while/body/eval_jaxpr/ppermute | solution.py:16
  260.6 11.1 %collective-permute-start.1 = (f32[1,8,128,128]{3,2,1,0:T(8,128)}, f32[1,8,128,128]{3,2,1,0:T(8,128)}, u32[]{:S(2)}, u32[]{:S(2)}) collective-permute-start(f32[1,8,128,128]{3,2,1,0:T(8,128)} %get-tuple-element.330), channel_id=1, source_target_pairs={{0,1},{1,2},{2,3},{3,4},{4,5},{5,6},{6,7},{7,8},{8,9},{9,10},{10,1... | collective-permute-start | bytes 1572872 | tf_op jit(solution)/shard_map/while/body/eval_jaxpr/ppermute | solution.py:16
  265.0 12.8 %collective-permute-start = (f32[1,8,128,128]{3,2,1,0:T(8,128)S(1)}, f32[1,8,128,128]{3,2,1,0:T(8,128)S(1)}, u32[]{:S(2)}, u32[]{:S(2)}) collective-permute-start(f32[1,8,128,128]{3,2,1,0:T(8,128)S(1)} %get-tuple-element.329), channel_id=1, source_target_pairs={{0,1},{1,2},{2,3},{3,4},{4,5},{5,6},{6,7},{7,8},{8,9},{9,10},{10,1... | collective-permute-start | bytes 1572872 | tf_op jit(solution)/shard_map/while/body/eval_jaxpr/ppermute | solution.py:16
  277.8 2.5 copy-start.1
  280.3 11.1 %collective-permute-start.1 = (f32[1,8,128,128]{3,2,1,0:T(8,128)}, f32[1,8,128,128]{3,2,1,0:T(8,128)}, u32[]{:S(2)}, u32[]{:S(2)}) collective-permute-start(f32[1,8,128,128]{3,2,1,0:T(8,128)} %get-tuple-element.330), channel_id=1, source_target_pairs={{0,1},{1,2},{2,3},{3,4},{4,5},{5,6},{6,7},{7,8},{8,9},{9,10},{10,1... | collective-permute-start | bytes 1572872 | tf_op jit(solution)/shard_map/while/body/eval_jaxpr/ppermute | solution.py:16
  284.7 12.8 %collective-permute-start = (f32[1,8,128,128]{3,2,1,0:T(8,128)S(1)}, f32[1,8,128,128]{3,2,1,0:T(8,128)S(1)}, u32[]{:S(2)}, u32[]{:S(2)}) collective-permute-start(f32[1,8,128,128]{3,2,1,0:T(8,128)S(1)} %get-tuple-element.329), channel_id=1, source_target_pairs={{0,1},{1,2},{2,3},{3,4},{4,5},{5,6},{6,7},{7,8},{8,9},{9,10},{10,1... | collective-permute-start | bytes 1572872 | tf_op jit(solution)/shard_map/while/body/eval_jaxpr/ppermute | solution.py:16
  300.1 11.1 %collective-permute-start.1 = (f32[1,8,128,128]{3,2,1,0:T(8,128)}, f32[1,8,128,128]{3,2,1,0:T(8,128)}, u32[]{:S(2)}, u32[]{:S(2)}) collective-permute-start(f32[1,8,128,128]{3,2,1,0:T(8,128)} %get-tuple-element.330), channel_id=1, source_target_pairs={{0,1},{1,2},{2,3},{3,4},{4,5},{5,6},{6,7},{7,8},{8,9},{9,10},{10,1... | collective-permute-start | bytes 1572872 | tf_op jit(solution)/shard_map/while/body/eval_jaxpr/ppermute | solution.py:16
  304.5 12.8 %collective-permute-start = (f32[1,8,128,128]{3,2,1,0:T(8,128)S(1)}, f32[1,8,128,128]{3,2,1,0:T(8,128)S(1)}, u32[]{:S(2)}, u32[]{:S(2)}) collective-permute-start(f32[1,8,128,128]{3,2,1,0:T(8,128)S(1)} %get-tuple-element.329), channel_id=1, source_target_pairs={{0,1},{1,2},{2,3},{3,4},{4,5},{5,6},{6,7},{7,8},{8,9},{9,10},{10,1... | collective-permute-start | bytes 1572872 | tf_op jit(solution)/shard_map/while/body/eval_jaxpr/ppermute | solution.py:16
  319.9 6.3 copy-start.6
  324.1 2.7 copy-start.2
  346.7 6.3 copy-start.6
  350.9 2.7 copy-start.2
  373.4 6.3 copy-start.6
  377.7 2.7 copy-start.2
  400.2 6.3 copy-start.6
  404.5 2.8 copy-start.2
  427.0 6.3 copy-start.6
  431.3 2.7 copy-start.2
  453.8 6.3 copy-start.6
  458.1 2.7 copy-start.2
  480.6 6.3 copy-start.6
  484.9 2.7 copy-start.2
  507.4 6.3 copy-start.6
  511.7 2.7 copy-start.2
  541.0 105.6 %copy-start.7 = (bf16[8,512,128]{2,1,0:T(8,128)(2,1)S(1)}, bf16[8,512,128]{2,1,0:T(8,128)(2,1)}, u32[]{:S(2)}) copy-start(bf16[8,512,128]{2,1,0:T(8,128)(2,1)} %get-tuple-element.103) | copy-start | bytes 3145732
  541.1 178.9 %reduce-scatter.5.cloned.1.call-start = ((), (), s32[]{:S(2)}) async-start(), calls=%async_computation.3 | async-start | bytes 589824 | tf_op jit(solution)/shard_map/reduce_scatter | solution.py:151
  (5 other events, 11.0 us)
Sparse Core Ops, SparseCore 0:
  541.2 105.4 reduce-scatter.2
  650.8 69.1 reduce-scatter.4
where the time goes:
time: 731 us; the launch traced here: 727 us
  waiting for transfers between devices  286 us (39%)
  matrix products  180 us (25%)
  starting transfers between devices  144 us (20%)
  other arithmetic  70.3 us (10%)
  local copies, waits for them, and re-layouts  30.8 us (4%)
  between operations  14.2 us (2%)
    ppermute x30, starting transfers between devices, passed_along(): lax.ppermute(value, axis, [(source, source + steps) for source in range(i...  144 us
    ppermute x30, waiting for transfers between devices, passed_along(): lax.ppermute(value, axis, [(source, source + steps) for source in range(i...  108 us
    reduce_scatter x1, waiting for transfers between devices, per_device(): lax.psum_scatter(terms, 'seq', scatter_dimension=1, tiled=True)  106 us
    dot_general x72, matrix products, product(): return jnp.dot(left, right, precision=exact_mode)  89.8 us
    reduce_scatter x1, waiting for transfers between devices, per_device(): lax.psum_scatter(partial_sum, 'dp', scatter_dimension=0, tiled=True)  72.1 us
    dot_general x122, matrix products, mixed_product(): jnp.dot(left, right, precision=split_mode, preferred_element_type=jnp.flo...  68.2 us
    add x15, other arithmetic, hand_over(): widened * incoming[1] + memory_local  38 us
    div x16, other arithmetic, chebyshev(): step_size = 1.0 / (center - momentum / step_size)  15.7 us
  transfers between devices with their start and end apart: 32, of which 24 were waited for; matrix products, arithmetic and copies ran while one was open for 0% of the time, Pallas kernels for 0%

commit v1 on v0

v1 whole, which is shorter than its diff:
```python
import functools

import jax
import jax.numpy as jnp
from jax import lax
from jax.experimental import pallas as pl
from jax.experimental.pallas import tpu as pltpu
from jax.sharding import PartitionSpec as P

F32 = jnp.float32
BF16 = jnp.bfloat16
MESH = pl.DeviceIdType.MESH

H = 8
C = 128
S = 4
ROWS = S * C
D = 2048
MSG = C + 8
ITERS = 4


def dot(a, b):
    return lax.dot_general(a, b, (((1,), (0,)), ((), ())), preferred_element_type=F32)


def dot_nt(a, b):
    return lax.dot_general(a, b, (((1,), (1,)), ((), ())), preferred_element_type=F32)


def dot_tn(a, b):
    return lax.dot_general(a, b, (((0,), (0,)), ((), ())), preferred_element_type=F32)


def kernel(
    tok_hbm, wq_hbm, k_hbm, v_hbm, ld_ref, reg_ref, g_hbm,
    mixed_hbm, qg_ref,
    tok, wq, kb, vb, gb, qb, mx,
    bs, el, wl, tl, ul, ll,
    loc, sib, tot, inbox, pre, pin, snd, st,
    gp, gin, zc, za, fin,
    load_sem, out_sem,
    sib_send, sib_recv, fw_send, fw_recv, bk_send, bk_recv, st_send, st_recv,
    gs_send, gs_recv, zc_send, zc_recv, za_send, za_recv, fin_send, fin_recv,
):
    dp = lax.axis_index("dp")
    seq = lax.axis_index("seq")
    core = lax.rem(seq, 2)
    other = 1 - core
    chip = lax.div(seq, 2)
    zpos = lax.div(chip, 2)
    ylo = lax.rem(chip, 2)
    twin = (dp, chip * 2 + other)

    def at_chip(c):
        return (dp, c * 2 + core)

    def at_z(z):
        return (dp, (z * 2 + ylo) * 2 + core)

    z_up = lax.rem(zpos + 1, 4)
    z_down = lax.rem(zpos + 3, 4)
    z_far = lax.rem(zpos + 2, 4)

    def remote(src, dst, send, recv, device):
        return pltpu.make_async_remote_copy(
            src_ref=src, dst_ref=dst, send_sem=send, recv_sem=recv, device_id=device, device_id_type=MESH
        )

    loads = [
        pltpu.make_async_copy(src, dst, load_sem.at[n])
        for n, (src, dst) in enumerate(
            ((k_hbm, kb), (v_hbm, vb), (wq_hbm, wq), (tok_hbm, tok), (g_hbm, gb))
        )
    ]
    for copy in loads:
        copy.start()

    barrier = pltpu.get_barrier_semaphore()
    pl.semaphore_signal(barrier, inc=1, device_id=twin, device_id_type=MESH)
    for n in range(1, 8):
        pl.semaphore_signal(barrier, inc=1, device_id=at_chip(lax.rem(chip + n, 8)), device_id_type=MESH)
    for n in range(1, 8):
        to = lax.rem(dp + n, 8)
        for y in range(2):
            pl.semaphore_signal(barrier, inc=1, device_id=(to, (zpos * 2 + y) * 2 + core), device_id_type=MESH)

    row_at = lax.broadcasted_iota(jnp.int32, (C, C), 0)
    col_at = lax.broadcasted_iota(jnp.int32, (C, C), 1)
    lower = row_at >= col_at
    eye = row_at == col_at

    def lanes(h):
        return pl.ds(pl.multiple_of(h * C, C), C)

    upper_ones = jnp.where(row_at <= col_at, 1.0, 0.0).astype(F32)
    for s in range(S):
        sums = lax.dot_general(
            ld_ref[:, s * C : (s + 1) * C], upper_ones, (((1,), (0,)), ((), ())),
            precision=lax.Precision.HIGHEST, preferred_element_type=F32,
        )
        for h in range(H):
            bs[h, s : s + 1, :] = sums[h : h + 1, :]

    loads[0].wait()
    loads[1].wait()

    def local_states(h, carry):
        m_sum = g_sum = None
        decay = None
        for s in range(S):
            rows = slice(s * C, (s + 1) * C)
            across = jnp.broadcast_to(bs[h, s : s + 1, :], (C, C))
            down = across.T
            e = jnp.exp(down)
            el[h, s] = e
            tail = jnp.exp(down[C - 1 : C, :] - down)
            k = kb[rows, lanes(h)]
            kt = (k.astype(F32) * tail).astype(BF16)
            vt = (vb[rows, lanes(h)].astype(F32) * tail).astype(BF16)
            m_new = dot_tn(vt, k)
            g_new = dot_tn(kt, k)
            ll[h, s, 0:C, :] = m_new
            ll[h, s, C : 2 * C, :] = g_new
            last = e[C - 1 : C, :]
            if s == 0:
                m_sum, g_sum, decay = m_new, g_new, last
            else:
                m_sum = last * m_sum + m_new
                g_sum = last * g_sum + g_new
                decay = decay * last
        tile = jnp.broadcast_to(decay, (8, C))
        loc[0, h, 0:C, :] = m_sum
        loc[0, h, C:MSG, :] = tile
        loc[1, h, 0:C, :] = g_sum
        loc[1, h, C:MSG, :] = tile
        return carry

    lax.fori_loop(0, H, local_states, 0)

    pl.semaphore_wait(barrier, 22)

    to_twin = remote(loc.at[other], sib, sib_send.at[0], sib_recv.at[0], twin)
    to_twin.start()

    loads[4].wait()

    def tables(h, carry):
        for s in range(S):
            rows = slice(s * C, (s + 1) * C)
            across = jnp.broadcast_to(bs[h, s : s + 1, :], (C, C))
            w = jnp.where(lower, jnp.exp(jnp.where(lower, across.T - across, 0.0)), 0.0)
            wl[h, s] = w
            k = kb[rows, lanes(h)]
            kf = k.astype(F32)
            square = jnp.broadcast_to(jnp.sum(kf * kf, axis=1, keepdims=True), (C, C))
            high = square.astype(BF16)
            low = (square - high.astype(F32)).astype(BF16)
            wb = w.astype(BF16)
            tl[h, s] = dot(jnp.concatenate([wb, wb], axis=1), jnp.concatenate([high, low], axis=0))
            ul[h, s] = (w * dot_nt(gb[rows, lanes(h)], vb[rows, lanes(h)])).astype(BF16)
        return carry

    lax.fori_loop(0, H // 2, tables, 0)

    to_twin.wait_recv()

    def total(h):
        mine_at = loc[core, h, C:MSG, :]
        sib_at = sib[h, C:MSG, :]
        first = core == 0
        by_mine = jnp.where(first, sib_at, 1.0)
        by_sib = jnp.where(first, 1.0, mine_at)
        tot[h, C:MSG, :] = mine_at * sib_at
        mine = loc[core, h, 0:C, :].reshape(C // 8, 8, C)
        theirs = sib[h, 0:C, :].reshape(C // 8, 8, C)
        tot[h, 0:C, :] = (by_mine[None] * mine + by_sib[None] * theirs).reshape(C, C)

    def forward(h):
        return remote(tot.at[h], inbox.at[chip], fw_send.at[h], fw_recv.at[chip], at_chip(h))

    def send_total(n, carry):
        h = lax.rem(chip + n, 8)
        total(h)
        forward(h).start()
        return carry

    lax.fori_loop(1, 8, send_total, 0)
    total(chip)
    inbox[chip] = tot[chip]

    lax.fori_loop(H // 2, H, tables, 0)

    loads[2].wait()
    loads[3].wait()
    for n in range(H // 2):
        block = dot(tok[...], wq[:, n * 2 * C : (n + 1) * 2 * C]).astype(BF16)
        qb[2 * n] = block[:, 0:C]
        qb[2 * n + 1] = block[:, C : 2 * C]

    def back(c):
        return remote(pre.at[c], pin.at[chip], bk_send.at[c], bk_recv.at[chip], at_chip(c))

    state = jnp.zeros((C // 8, 8, C), F32)
    for c in range(8):
        pre[c] = state.reshape(C, C)

        @pl.when(c != chip)
        def _():
            back(c).start()
            remote(tot.at[c], inbox.at[c], fw_send.at[c], fw_recv.at[c], at_chip(c)).wait_recv()

        state = inbox[c, C:MSG, :][None] * state + inbox[c, 0:C, :].reshape(C // 8, 8, C)
    pin[chip] = pre[chip]

    def hand_over(h):
        return remote(snd.at[h], st.at[core, h], st_send.at[h], st_recv.at[h], twin)

    def spread(n, carry):
        h = lax.rem(dp + 1 + n, 8)

        @pl.when(h != chip)
        def _():
            remote(pre.at[h], pin.at[h], bk_send.at[h], bk_recv.at[h], at_chip(h)).wait_recv()

        base = pin[h].reshape(C // 8, 8, C)
        mine_at = loc[core, h, C:MSG, :]
        sib_at = sib[h, C:MSG, :]
        mine = mine_at[None] * base + loc[core, h, 0:C, :].reshape(C // 8, 8, C)
        theirs = sib_at[None] * base + sib[h, 0:C, :].reshape(C // 8, 8, C)
        first = core == 0
        snd[h] = jnp.where(first, mine, base).reshape(C, C)
        st[core, h] = jnp.where(first, base, theirs).reshape(C, C)
        hand_over(h).start()
        return carry

    lax.fori_loop(0, H, spread, 0)

    def apply(pq, pg, e, w, state, k):
        p = jnp.concatenate([pq, pg], axis=0).astype(BF16)
        scores = dot_nt(p, k)
        left = jnp.concatenate(
            [
                jnp.concatenate([e * pq, e * pg], axis=0).astype(BF16),
                jnp.concatenate([w * scores[0:C], w * scores[C : 2 * C]], axis=0).astype(BF16),
            ],
            axis=1,
        )
        y = dot(left, jnp.concatenate([state, k], axis=0))
        return y[0:C], y[C : 2 * C]

    def solve(n):
        h = lax.rem(dp + 1 + n, 8)
        ridge = reg_ref[h]
        remote(snd.at[h], st.at[other, h], st_send.at[h], st_recv.at[h], twin).wait_recv()
        m, g = st[0, h], st[1, h]
        trace = jnp.sum(jnp.sum(jnp.where(eye, g, 0.0), axis=0, keepdims=True), axis=1, keepdims=True)
        trace = jnp.broadcast_to(trace, (1, C))
        each = []
        for s in range(S):
            rows = slice(s * C, (s + 1) * C)
            e, w = el[h, s], wl[h, s]
            spans = e * trace + tl[h, s]
            trace = spans[C - 1 : C, :]
            half = 0.5 * spans
            center = ridge + half
            square = half * half
            alpha = 1.0 / center
            alphas, betas = [alpha], [None]
            for step in range(1, ITERS):
                factor = 0.5 if step == 1 else 0.25
                betas.append(factor * (half * alpha) * (half * alpha))
                alpha = 1.0 / (center - factor * square * alpha)
                alphas.append(alpha)
            each.append(dict(rows=rows, e=e, w=w, m=m.astype(BF16), g=g.astype(BF16), a=alphas, b=betas))
            if s + 1 < S:
                last = e[C - 1 : C, :]
                m = last * m + ll[h, s, 0:C, :]
                g = last * g + ll[h, s, C : 2 * C, :]
        for s, t in enumerate(each):
            k = kb[t["rows"], lanes(h)]
            grad = gb[t["rows"], lanes(h)].astype(F32)
            left = jnp.concatenate([(t["e"] * grad).astype(BF16), ul[h, s]], axis=1)
            rg = dot(left, jnp.concatenate([t["m"], k], axis=0))
            rq = qb[h, t["rows"], :].astype(F32)
            t.update(k=k, rq=rq, rg=rg, pq=rq, pg=rg, xq=t["a"][0] * rq, xg=t["a"][0] * rg)
        for step in range(1, ITERS):
            for t in each:
                yq, yg = apply(t["pq"], t["pg"], t["e"], t["w"], t["g"], t["k"])
                before, now, beta = t["a"][step - 1], t["a"][step], t["b"][step]
                for i, y in (("q", yq), ("g", yg)):
                    res = t["r" + i] - before * (ridge * t["p" + i] + y)
                    p = res + beta * t["p" + i]
                    t["r" + i], t["p" + i] = res, p
                    t["x" + i] = t["x" + i] + now * p
        solved = []
        for s, t in enumerate(each):
            scores = dot_nt(t["xq"].astype(BF16), t["k"])
            y = dot_nt((t["e"] * t["xq"]).astype(BF16), t["m"])
            y = y + dot((t["w"] * scores).astype(BF16), vb[t["rows"], lanes(h)])
            mx[t["rows"], lanes(h)] = y.astype(BF16)
            solved.append(t["xg"].T.astype(BF16))
        left = jnp.concatenate(solved, axis=1)
        for c in range(8):
            part = dot(left, tok[:, c * 2 * C : (c + 1) * 2 * C])
            gp[n, 0, c] = part[:, 0:C]
            gp[n, 1, c] = part[:, C : 2 * C]

    def out_copy(n):
        h = lax.rem(dp + 1 + n, 8)
        return pltpu.make_async_copy(mx.at[:, lanes(h)], mixed_hbm.at[:, lanes(h)], out_sem.at[n])

    def to_core(n):
        return remote(gp.at[n, other], gin.at[n], gs_send.at[n], gs_recv.at[n], twin)

    def far_up(n):
        return remote(gp.at[n, core, z_far * 2], zc.at[n, 0], zc_send.at[n, 0], zc_recv.at[n, 0], at_z(z_up))

    def far_down(n):
        return remote(gp.at[n, core, z_far * 2 + 1], zc.at[n, 1], zc_send.at[n, 1], zc_recv.at[n, 1], at_z(z_down))

    def near_up(n):
        return remote(gp.at[n, core, pl.ds(z_up * 2, 2)], za.at[n, 0], za_send.at[n, 0], za_recv.at[n, 0], at_z(z_up))

    def near_down(n):
        return remote(
            gp.at[n, core, pl.ds(z_down * 2, 2)], za.at[n, 1], za_send.at[n, 1], za_recv.at[n, 1], at_z(z_down)
        )

    def finish(n, y):
        h = lax.rem(dp + 1 + n, 8)
        return remote(
            gp.at[n, core, zpos * 2 + y], fin.at[dp * 2 + ylo], fin_send.at[n, y], fin_recv.at[dp * 2 + ylo],
            (h, (zpos * 2 + y) * 2 + core),
        )

    def turn(i, carry):
        @pl.when(i < H)
        def _():
            solve(i)
            to_core(i).start()
            out_copy(i).start()

        @pl.when((i >= 1) & (i < H + 1))
        def _():
            n = i - 1
            to_core(n).wait_recv()
            gp[n, core] = gp[n, core] + gin[n]
            far_up(n).start()
            far_down(n).start()

        @pl.when((i >= 2) & (i < H + 2))
        def _():
            n = i - 2
            far_up(n).wait_recv()
            far_down(n).wait_recv()
            gp[n, core, z_up * 2] = gp[n, core, z_up * 2] + zc[n, 0]
            gp[n, core, z_down * 2 + 1] = gp[n, core, z_down * 2 + 1] + zc[n, 1]
            near_up(n).start()
            near_down(n).start()

        @pl.when((i >= 3) & (i < H + 3))
        def _():
            n = i - 3
            near_up(n).wait_recv()
            near_down(n).wait_recv()
            for y in range(2):
                gp[n, core, zpos * 2 + y] = gp[n, core, zpos * 2 + y] + za[n, 0, y] + za[n, 1, y]

                @pl.when((n < H - 1) | (ylo != y))
                def _():
                    finish(n, y).start()

                @pl.when((n == H - 1) & (ylo == y))
                def _():
                    fin[dp * 2 + y] = gp[n, core, zpos * 2 + y]

        return carry

    lax.fori_loop(0, H + 3, turn, 0)

    acc = None
    for source in range(16):

        @pl.when(dp * 2 + ylo != source)
        def _():
            remote(
                gp.at[0, core, 0], fin.at[source], fin_send.at[0, 0], fin_recv.at[source], twin
            ).wait_recv()

        acc = fin[source] if acc is None else acc + fin[source]
    qg_ref[...] = acc

    to_twin.wait_send()

    def drain(n, carry):
        @pl.when(n != chip)
        def _():
            forward(n).wait_send()
            back(n).wait_send()

        hand_over(n).wait_send()
        out_copy(n).wait()
        to_core(n).wait_send()
        far_up(n).wait_send()
        far_down(n).wait_send()
        near_up(n).wait_send()
        near_down(n).wait_send()
        for y in range(2):

            @pl.when((n < H - 1) | (ylo != y))
            def _():
                finish(n, y).wait_send()

        return carry

    lax.fori_loop(0, H, drain, 0)


def per_device(tokens, w_query, keys, values, log_decay, regular, grad_out):
    dma = pltpu.SemaphoreType.DMA
    hbm = pl.BlockSpec(memory_space=pl.ANY)
    vmem = pl.BlockSpec(memory_space=pltpu.VMEM)
    smem = pl.BlockSpec(memory_space=pltpu.SMEM)
    mixed, query_grad = pl.pallas_call(
        kernel,
        out_shape=(
            jax.ShapeDtypeStruct((ROWS, H * C), BF16),
            jax.ShapeDtypeStruct((C, C), F32),
        ),
        in_specs=[hbm, hbm, hbm, hbm, vmem, smem, hbm],
        out_specs=(hbm, vmem),
        scratch_shapes=[
            pltpu.VMEM((ROWS, D), BF16),
            pltpu.VMEM((D, H * C), BF16),
            pltpu.VMEM((ROWS, H * C), BF16),
            pltpu.VMEM((ROWS, H * C), BF16),
            pltpu.VMEM((ROWS, H * C), BF16),
            pltpu.VMEM((H, ROWS, C), BF16),
            pltpu.VMEM((ROWS, H * C), BF16),
            pltpu.VMEM((H, S, C), F32),
            pltpu.VMEM((H, S, C, C), F32),
            pltpu.VMEM((H, S, C, C), F32),
            pltpu.VMEM((H, S, C, C), F32),
            pltpu.VMEM((H, S, C, C), BF16),
            pltpu.VMEM((H, S, 2 * C, C), F32),
            pltpu.VMEM((2, H, MSG, C), F32),
            pltpu.VMEM((H, MSG, C), F32),
            pltpu.VMEM((H, MSG, C), F32),
            pltpu.VMEM((H, MSG, C), F32),
            pltpu.VMEM((H, C, C), F32),
            pltpu.VMEM((H, C, C), F32),
            pltpu.VMEM((H, C, C), F32),
            pltpu.VMEM((2, H, C, C), F32),
            pltpu.VMEM((H, 2, 8, C, C), F32),
            pltpu.VMEM((H, 8, C, C), F32),
            pltpu.VMEM((H, 2, C, C), F32),
            pltpu.VMEM((H, 2, 2, C, C), F32),
            pltpu.VMEM((16, C, C), F32),
            dma((5,)),
            dma((H,)),
            dma((1,)),
            dma((1,)),
            dma((H,)),
            dma((H,)),
            dma((H,)),
            dma((H,)),
            dma((H,)),
            dma((H,)),
            dma((H,)),
            dma((H,)),
            dma((H, 2)),
            dma((H, 2)),
            dma((H, 2)),
            dma((H, 2)),
            dma((H, 2)),
            dma((16,)),
        ],
        compiler_params=pltpu.CompilerParams(
            collective_id=0, has_side_effects=True, vmem_limit_bytes=60 * 2**20
        ),
    )(
        tokens.reshape(ROWS, D),
        w_query,
        keys.reshape(ROWS, H * C),
        values.reshape(ROWS, H * C),
        log_decay.reshape(H, ROWS),
        regular,
        grad_out.reshape(ROWS, H * C),
    )
    return mixed.reshape(1, ROWS, H * C), query_grad


def solution(mesh):
    in_specs = (
        P("dp", "seq", None),
        P(),
        P("dp", "seq", None),
        P("dp", "seq", None),
        P("dp", None, "seq"),
        P(),
        P("dp", "seq", None),
    )
    out_specs = (P("dp", "seq", None), P("dp", "seq"))
    return jax.shard_map(
        per_device, mesh=mesh, in_specs=in_specs, out_specs=out_specs, check_vma=False
    )
```

time: 731 us -> 81.9 us (0.11)
  the two profiles are of different devices: /device:TPU:1 before, /device:TPU:22 now
where the time goes in v1:
time: 81.9 us; the launch traced here: 81.7 us
  Pallas kernels  77.3 us (94%)
  local copies, waits for them, and re-layouts  3.74 us (5%)
    pallas_call x1, Pallas kernels, per_device(): pl.pallas_call(kernel, out_shape=(jax.ShapeDtypeStruct((ROWS, H * C), BF1...  77.3 us
    unnamed x2, local copies, waits for them, and re-layouts  3.74 us

profile of v1, /device:TPU:22, one launch (start us, length us, event | category | flops | bytes accessed | tf_op | source)
XLA Modules:
  0.0 81.7 jit_solution(5559234603956628741)
XLA Ops:
  0.6 77.3 %shard_map.86 = (bf16[512,1024]{1,0:T(8,128)(2,1)}, f32[128,128]{1,0:T(8,128)}) custom-call(bf16[512,2048]{1,0:T(8,128)(2,1)} %bitcast.6, bf16[2048,1024]{1,0:T(8,128)(2,1)} %wq_hbm.1, bf16[512,1024]{1,0:T(8,128)(2,1)} %bitcast.7, bf16[512,1024]{1,0:T(8,128)(2,1)} %bitcast.8, f32[8,512]{1,0:T(8,128)} %bitcast.11, f32[8]{0:T(128)} %reg_ref.1, ...), custom_call_target="tpu_custom_call" | custom-call | tf_op jit(solution)/shard_map/pallas_call | solution.py:425
  77.9 2.3 %copy.11 = bf16[1,512,1024]{2,1,0:T(8,128)(2,1)} copy(bf16[1,512,1024]{2,1,0:T(8,128)(2,1)} %bitcast.10) | data formatting | bytes 2097152
  80.2 1.5 %copy.12 = f32[128,128]{1,0:T(8,128)} copy(f32[128,128]{1,0:T(8,128)} %get-tuple-element.9) | data formatting | bytes 131072

commit v2 on v1

--- a/solution.py
+++ b/solution.py
@@ -38,7 +38,7 @@
     tok, wq, kb, vb, gb, qb, mx,
     bs, el, wl, tl, ul, ll,
     loc, sib, tot, inbox, pre, pin, snd, st,
-    gp, gin, zc, za, fin,
+    gp, gin, zc, za, ya, fin,
     load_sem, out_sem,
     sib_send, sib_recv, fw_send, fw_recv, bk_send, bk_recv, st_send, st_recv,
     gs_send, gs_recv, zc_send, zc_recv, za_send, za_recv, fin_send, fin_recv,
@@ -80,15 +80,35 @@
     pl.semaphore_signal(barrier, inc=1, device_id=twin, device_id_type=MESH)
     for n in range(1, 8):
         pl.semaphore_signal(barrier, inc=1, device_id=at_chip(lax.rem(chip + n, 8)), device_id_type=MESH)
-    for n in range(1, 8):
-        to = lax.rem(dp + n, 8)
-        for y in range(2):
-            pl.semaphore_signal(barrier, inc=1, device_id=(to, (zpos * 2 + y) * 2 + core), device_id_type=MESH)
+    near_same = (dp, (zpos * 2 + 1 - ylo) * 2 + core)
+    near_other = (dp + 1 - 2 * lax.rem(dp, 2), (zpos * 2 + 1 - ylo) * 2 + core)
+
+    def greet(device):
+        pl.semaphore_signal(barrier, inc=1, device_id=device, device_id_type=MESH)
+
+    @pl.when(core == 0)
+    def _():
+        for n in range(1, 8):
+            for y in range(2):
+                greet((lax.rem(dp + n, 8), (zpos * 2 + y) * 2))
+
+    @pl.when(core == 1)
+    def _():
+        greet(near_other)
+        for n in range(1, 4):
+            for z in range(4):
+                greet((lax.rem(dp + 2 * n, 8), (z * 2 + ylo) * 2 + 1))
 
     row_at = lax.broadcasted_iota(jnp.int32, (C, C), 0)
     col_at = lax.broadcasted_iota(jnp.int32, (C, C), 1)
     lower = row_at >= col_at
     eye = row_at == col_at
+
+    xpos = lax.div(dp, 2)
+    yhi = lax.rem(dp, 2)
+
+    def head_at(n):
+        return 2 * lax.rem(xpos + 1 + lax.div(n, 2), 4) + lax.rem(yhi + 1 + n, 2)
 
     def lanes(h):
         return pl.ds(pl.multiple_of(h * C, C), C)
@@ -138,7 +158,7 @@
 
     lax.fori_loop(0, H, local_states, 0)
 
-    pl.semaphore_wait(barrier, 22)
+    pl.semaphore_wait(barrier, jnp.where(core == 0, 22, 21))
 
     to_twin = remote(loc.at[other], sib, sib_send.at[0], sib_recv.at[0], twin)
     to_twin.start()
@@ -217,7 +237,7 @@
         return remote(snd.at[h], st.at[core, h], st_send.at[h], st_recv.at[h], twin)
 
     def spread(n, carry):
-        h = lax.rem(dp + 1 + n, 8)
+        h = head_at(n)
 
         @pl.when(h != chip)
         def _():
@@ -250,7 +270,7 @@
         return y[0:C], y[C : 2 * C]
 
     def solve(n):
-        h = lax.rem(dp + 1 + n, 8)
+        h = head_at(n)
         ridge = reg_ref[h]
         remote(snd.at[h], st.at[other, h], st_send.at[h], st_recv.at[h], twin).wait_recv()
         m, g = st[0, h], st[1, h]
@@ -303,36 +323,61 @@
         left = jnp.concatenate(solved, axis=1)
         for c in range(8):
             part = dot(left, tok[:, c * 2 * C : (c + 1) * 2 * C])
-            gp[n, 0, c] = part[:, 0:C]
-            gp[n, 1, c] = part[:, C : 2 * C]
+            gp[n, 0, c // 2, c % 2] = part[:, 0:C]
+            gp[n, 1, c // 2, c % 2] = part[:, C : 2 * C]
 
     def out_copy(n):
-        h = lax.rem(dp + 1 + n, 8)
+        h = head_at(n)
         return pltpu.make_async_copy(mx.at[:, lanes(h)], mixed_hbm.at[:, lanes(h)], out_sem.at[n])
 
     def to_core(n):
         return remote(gp.at[n, other], gin.at[n], gs_send.at[n], gs_recv.at[n], twin)
 
     def far_up(n):
-        return remote(gp.at[n, core, z_far * 2], zc.at[n, 0], zc_send.at[n, 0], zc_recv.at[n, 0], at_z(z_up))
+        return remote(gp.at[n, 0, z_far, 0], zc.at[n, 0], zc_send.at[n, 0], zc_recv.at[n, 0], at_z(z_up))
 
     def far_down(n):
-        return remote(gp.at[n, core, z_far * 2 + 1], zc.at[n, 1], zc_send.at[n, 1], zc_recv.at[n, 1], at_z(z_down))
+        return remote(gp.at[n, 0, z_far, 1], zc.at[n, 1], zc_send.at[n, 1], zc_recv.at[n, 1], at_z(z_down))
 
     def near_up(n):
-        return remote(gp.at[n, core, pl.ds(z_up * 2, 2)], za.at[n, 0], za_send.at[n, 0], za_recv.at[n, 0], at_z(z_up))
+        return remote(gp.at[n, 0, z_up], za.at[n, 0], za_send.at[n, 0], za_recv.at[n, 0], at_z(z_up))
 
     def near_down(n):
+        return remote(gp.at[n, 0, z_down], za.at[n, 1], za_send.at[n, 1], za_recv.at[n, 1], at_z(z_down))
+
+    def finish_z(n, y):
+        at = dp * 2 + ylo
         return remote(
-            gp.at[n, core, pl.ds(z_down * 2, 2)], za.at[n, 1], za_send.at[n, 1], za_recv.at[n, 1], at_z(z_down)
-        )
-
-    def finish(n, y):
-        h = lax.rem(dp + 1 + n, 8)
+            gp.at[n, 0, zpos, y], fin.at[at], fin_send.at[n, y], fin_recv.at[at], (head_at(n), (zpos * 2 + y) * 2)
+        )
+
+    def far_same(n):
         return remote(
-            gp.at[n, core, zpos * 2 + y], fin.at[dp * 2 + ylo], fin_send.at[n, y], fin_recv.at[dp * 2 + ylo],
-            (h, (zpos * 2 + y) * 2 + core),
-        )
+            gp.at[n, 1, 0:2, ylo], zc.at[n], zc_send.at[n, 0], zc_recv.at[n, 0], near_same
+        )
+
+    def far_other(n):
+        return remote(
+            gp.at[n, 1, 2:4, ylo], zc.at[n + 1], zc_send.at[n, 1], zc_recv.at[n, 1], near_other
+        )
+
+    def send_other(n):
+        return remote(gp.at[n, 1, :, 1 - ylo], ya.at[n], za_send.at[n, 0], za_recv.at[n, 0], near_other)
+
+    def send_same(n):
+        return remote(gp.at[n, 1, :, 1 - ylo], ya.at[n], za_send.at[n, 0], za_recv.at[n, 0], near_same)
+
+    def finish_y(n, z):
+        at = xpos * 4 + zpos
+        return remote(
+            gp.at[n, 1, z, ylo], fin.at[at], fin_send.at[n, z], fin_recv.at[at], (head_at(n), (z * 2 + ylo) * 2 + 1)
+        )
+
+    def odd(n):
+        return lax.rem(n, 2) == 1
+
+    def even(n):
+        return lax.rem(n, 2) == 0
 
     def turn(i, carry):
         @pl.when(i < H)
@@ -341,52 +386,88 @@
             to_core(i).start()
             out_copy(i).start()
 
-        @pl.when((i >= 1) & (i < H + 1))
-        def _():
-            n = i - 1
-            to_core(n).wait_recv()
-            gp[n, core] = gp[n, core] + gin[n]
-            far_up(n).start()
-            far_down(n).start()
-
-        @pl.when((i >= 2) & (i < H + 2))
-        def _():
-            n = i - 2
-            far_up(n).wait_recv()
-            far_down(n).wait_recv()
-            gp[n, core, z_up * 2] = gp[n, core, z_up * 2] + zc[n, 0]
-            gp[n, core, z_down * 2 + 1] = gp[n, core, z_down * 2 + 1] + zc[n, 1]
-            near_up(n).start()
-            near_down(n).start()
-
-        @pl.when((i >= 3) & (i < H + 3))
-        def _():
-            n = i - 3
-            near_up(n).wait_recv()
-            near_down(n).wait_recv()
+        n1, n2, n3 = i - 1, i - 2, i - 3
+        in1 = (i >= 1) & (i < H + 1)
+        in2 = (i >= 2) & (i < H + 2)
+        in3 = (i >= 3) & (i < H + 3)
+
+        @pl.when(in1)
+        def _():
+            to_core(n1).wait_recv()
+            gp[n1, core] = gp[n1, core] + gin[n1]
+
+        @pl.when(in1 & (core == 0))
+        def _():
+            far_up(n1).start()
+            far_down(n1).start()
+
+        @pl.when(in2 & (core == 0))
+        def _():
+            far_up(n2).wait_recv()
+            far_down(n2).wait_recv()
+            gp[n2, 0, z_up, 0] = gp[n2, 0, z_up, 0] + zc[n2, 0]
+            gp[n2, 0, z_down, 1] = gp[n2, 0, z_down, 1] + zc[n2, 1]
+            near_up(n2).start()
+            near_down(n2).start()
+
+        @pl.when(in3 & (core == 0))
+        def _():
+            near_up(n3).wait_recv()
+            near_down(n3).wait_recv()
             for y in range(2):
-                gp[n, core, zpos * 2 + y] = gp[n, core, zpos * 2 + y] + za[n, 0, y] + za[n, 1, y]
-
-                @pl.when((n < H - 1) | (ylo != y))
+                gp[n3, 0, zpos, y] = gp[n3, 0, zpos, y] + za[n3, 0, y] + za[n3, 1, y]
+
+                @pl.when((n3 < H - 1) | (ylo != y))
                 def _():
-                    finish(n, y).start()
-
-                @pl.when((n == H - 1) & (ylo == y))
+                    finish_z(n3, y).start()
+
+                @pl.when((n3 == H - 1) & (ylo == y))
                 def _():
-                    fin[dp * 2 + y] = gp[n, core, zpos * 2 + y]
+                    fin[dp * 2 + y] = gp[n3, 0, zpos, y]
+
+        @pl.when(in1 & (core == 1) & even(n1))
+        def _():
+            far_same(n1).start()
+            far_other(n1).start()
+
+        @pl.when(in1 & (core == 1) & odd(n1))
+        def _():
+            far_other(n1 - 1).wait_recv()
+            gp[n1, 1, 2:4, 1 - ylo] = gp[n1, 1, 2:4, 1 - ylo] + zc[n1]
+            send_same(n1).start()
+
+        @pl.when(in2 & (core == 1) & even(n2))
+        def _():
+            far_same(n2).wait_recv()
+            gp[n2, 1, 0:2, 1 - ylo] = gp[n2, 1, 0:2, 1 - ylo] + zc[n2]
+            send_other(n2).start()
+
+        @pl.when(in3 & (core == 1) & odd(n3))
+        def _():
+            send_other(n3 - 1).wait_recv()
+            send_same(n3).wait_recv()
+            for z in range(4):
+                gp[n3, 1, z, ylo] = gp[n3, 1, z, ylo] + ya[n3 - 1, z] + ya[n3, z]
+
+                @pl.when((n3 < H - 1) | (zpos != z))
+                def _():
+                    finish_y(n3, z).start()
+
+                @pl.when((n3 == H - 1) & (zpos == z))
+                def _():
+                    fin[xpos * 4 + z] = gp[n3, 1, z, ylo]
 
         return carry
 
     lax.fori_loop(0, H + 3, turn, 0)
 
     acc = None
+    own = jnp.where(core == 0, dp * 2 + ylo, xpos * 4 + zpos)
     for source in range(16):
 
-        @pl.when(dp * 2 + ylo != source)
-        def _():
-            remote(
-                gp.at[0, core, 0], fin.at[source], fin_send.at[0, 0], fin_recv.at[source], twin
-            ).wait_recv()
+        @pl.when(own != source)
+        def _():
+            remote(gp.at[0, 0, 0, 0], fin.at[source], fin_send.at[0, 0], fin_recv.at[source], twin).wait_recv()
 
         acc = fin[source] if acc is None else acc + fin[source]
     qg_ref[...] = acc
@@ -402,15 +483,33 @@
         hand_over(n).wait_send()
         out_copy(n).wait()
         to_core(n).wait_send()
-        far_up(n).wait_send()
-        far_down(n).wait_send()
-        near_up(n).wait_send()
-        near_down(n).wait_send()
-        for y in range(2):
-
-            @pl.when((n < H - 1) | (ylo != y))
-            def _():
-                finish(n, y).wait_send()
+
+        @pl.when(core == 0)
+        def _():
+            far_up(n).wait_send()
+            far_down(n).wait_send()
+            near_up(n).wait_send()
+            near_down(n).wait_send()
+            for y in range(2):
+
+                @pl.when((n < H - 1) | (ylo != y))
+                def _():
+                    finish_z(n, y).wait_send()
+
+        @pl.when((core == 1) & even(n))
+        def _():
+            far_same(n).wait_send()
+            far_other(n).wait_send()
+            send_other(n).wait_send()
+
+        @pl.when((core == 1) & odd(n))
+        def _():
+            send_same(n).wait_send()
+            for z in range(4):
+
+                @pl.when((n < H - 1) | (zpos != z))
+                def _():
+                    finish_y(n, z).wait_send()
 
         return carry
 
@@ -452,10 +551,11 @@
             pltpu.VMEM((H, C, C), F32),
             pltpu.VMEM((H, C, C), F32),
             pltpu.VMEM((2, H, C, C), F32),
-            pltpu.VMEM((H, 2, 8, C, C), F32),
-            pltpu.VMEM((H, 8, C, C), F32),
+            pltpu.VMEM((H, 2, 4, 2, C, C), F32),
+            pltpu.VMEM((H, 4, 2, C, C), F32),
             pltpu.VMEM((H, 2, C, C), F32),
             pltpu.VMEM((H, 2, 2, C, C), F32),
+            pltpu.VMEM((H, 4, C, C), F32),
             pltpu.VMEM((16, C, C), F32),
             dma((5,)),
             dma((H,)),
@@ -473,7 +573,7 @@
             dma((H, 2)),
             dma((H, 2)),
             dma((H, 2)),
-            dma((H, 2)),
+            dma((H, 4)),
             dma((16,)),
         ],
         compiler_params=pltpu.CompilerParams(

time: 81.9 us -> 78.2 us (0.955)
  the two profiles are of different devices: /device:TPU:22 before, /device:TPU:1 now
where the time goes in v2:
time: 78.2 us; the launch traced here: 77.2 us
  Pallas kernels  72.8 us (93%)
  local copies, waits for them, and re-layouts  3.74 us (5%)
    pallas_call x1, Pallas kernels, per_device(): pl.pallas_call(kernel, out_shape=(jax.ShapeDtypeStruct((ROWS, H * C), BF1...  72.8 us
    unnamed x2, local copies, waits for them, and re-layouts  3.74 us

profile of v2, /device:TPU:1, one launch (start us, length us, event | category | flops | bytes accessed | tf_op | source)
XLA Modules:
  0.0 77.2 jit_solution(942322812522528711)
XLA Ops:
  0.6 72.8 %shard_map.86 = (bf16[512,1024]{1,0:T(8,128)(2,1)}, f32[128,128]{1,0:T(8,128)}) custom-call(bf16[512,2048]{1,0:T(8,128)(2,1)} %bitcast.6, bf16[2048,1024]{1,0:T(8,128)(2,1)} %wq_hbm.1, bf16[512,1024]{1,0:T(8,128)(2,1)} %bitcast.7, bf16[512,1024]{1,0:T(8,128)(2,1)} %bitcast.8, f32[8,512]{1,0:T(8,128)} %bitcast.11, f32[8]{0:T(128)} %reg_ref.1, ...), custom_call_target="tpu_custom_call" | custom-call | tf_op jit(solution)/shard_map/pallas_call | solution.py:524
  73.4 2.3 %copy.11 = bf16[1,512,1024]{2,1,0:T(8,128)(2,1)} copy(bf16[1,512,1024]{2,1,0:T(8,128)(2,1)} %bitcast.10) | data formatting | bytes 2097152
  75.7 1.5 %copy.12 = f32[128,128]{1,0:T(8,128)} copy(f32[128,128]{1,0:T(8,128)} %get-tuple-element.9) | data formatting | bytes 131072

commit v3 on v2

--- a/solution.py
+++ b/solution.py
@@ -17,7 +17,9 @@
 ROWS = S * C
 D = 2048
 MSG = C + 8
+HALF = C // 2
 ITERS = 4
+FAR, SAME, NEAR = 3, 2, 5
 
 
 def dot(a, b):
@@ -185,31 +187,85 @@
 
     to_twin.wait_recv()
 
-    def total(h):
+    def unit(r, u):
+        return head_at(4 * r + lax.div(u, 2)), pl.ds(pl.multiple_of(lax.rem(u, 2) * HALF, HALF), HALF)
+
+    def tiles(block):
+        return block.reshape(HALF // 8, 8, C)
+
+    def total(r, u):
+        h, half = unit(r, u)
         mine_at = loc[core, h, C:MSG, :]
         sib_at = sib[h, C:MSG, :]
         first = core == 0
         by_mine = jnp.where(first, sib_at, 1.0)
         by_sib = jnp.where(first, 1.0, mine_at)
-        tot[h, C:MSG, :] = mine_at * sib_at
-        mine = loc[core, h, 0:C, :].reshape(C // 8, 8, C)
-        theirs = sib[h, 0:C, :].reshape(C // 8, 8, C)
-        tot[h, 0:C, :] = (by_mine[None] * mine + by_sib[None] * theirs).reshape(C, C)
-
-    def forward(h):
-        return remote(tot.at[h], inbox.at[chip], fw_send.at[h], fw_recv.at[chip], at_chip(h))
-
-    def send_total(n, carry):
-        h = lax.rem(chip + n, 8)
-        total(h)
-        forward(h).start()
-        return carry
-
-    lax.fori_loop(1, 8, send_total, 0)
-    total(chip)
-    inbox[chip] = tot[chip]
+        tot[r, u, HALF : HALF + 8, :] = mine_at * sib_at
+        mine, theirs = tiles(loc[core, h, half, :]), tiles(sib[h, half, :])
+        tot[r, u, 0:HALF, :] = (by_mine[None] * mine + by_sib[None] * theirs).reshape(HALF, C)
+
+    def forward(r, u):
+        return remote(tot.at[r, u], inbox.at[r, chip], fw_send.at[r, u], fw_recv.at[r, chip], at_chip(u))
+
+    def send_totals(r):
+        def one(n, carry):
+            u = lax.rem(chip + n, 8)
+            total(r, u)
+            forward(r, u).start()
+            return carry
+
+        lax.fori_loop(1, 8, one, 0)
+        total(r, chip)
+        inbox[r, chip] = tot[r, chip]
+
+    def back(r, c):
+        return remote(pre.at[r, c], pin.at[r, chip], bk_send.at[r, c], bk_recv.at[r, chip], at_chip(c))
+
+    def prefix(r):
+        state = jnp.zeros((HALF // 8, 8, C), F32)
+        for c in range(8):
+            pre[r, c] = state.reshape(HALF, C)
+
+            @pl.when(c != chip)
+            def _():
+                back(r, c).start()
+                remote(tot.at[r, c], inbox.at[r, c], fw_send.at[r, c], fw_recv.at[r, c], at_chip(c)).wait_recv()
+
+            state = inbox[r, c, HALF : HALF + 8, :][None] * state + tiles(inbox[r, c, 0:HALF, :])
+        pin[r, chip] = pre[r, chip]
+
+    def hand_over(h):
+        return remote(snd.at[h], st.at[core, h], st_send.at[h], st_recv.at[h], twin)
+
+    def spread(r):
+        def one(e, carry):
+            h = head_at(4 * r + e)
+            mine_at = loc[core, h, C:MSG, :]
+            sib_at = sib[h, C:MSG, :]
+            first = core == 0
+            for part in range(2):
+                u = 2 * e + part
+                half = slice(part * HALF, (part + 1) * HALF)
+
+                @pl.when(u != chip)
+                def _():
+                    remote(pre.at[r, u], pin.at[r, u], bk_send.at[r, u], bk_recv.at[r, u], at_chip(u)).wait_recv()
+
+                base = tiles(pin[r, u])
+                mine = mine_at[None] * base + tiles(loc[core, h, half, :])
+                theirs = sib_at[None] * base + tiles(sib[h, half, :])
+                snd[h, half, :] = jnp.where(first, mine, base).reshape(HALF, C)
+                st[core, h, half, :] = jnp.where(first, base, theirs).reshape(HALF, C)
+            hand_over(h).start()
+            return carry
+
+        lax.fori_loop(0, 4, one, 0)
+
+    send_totals(0)
 
     lax.fori_loop(H // 2, H, tables, 0)
+
+    prefix(0)
 
     loads[2].wait()
     loads[3].wait()
@@ -218,43 +274,8 @@
         qb[2 * n] = block[:, 0:C]
         qb[2 * n + 1] = block[:, C : 2 * C]
 
-    def back(c):
-        return remote(pre.at[c], pin.at[chip], bk_send.at[c], bk_recv.at[chip], at_chip(c))
-
-    state = jnp.zeros((C // 8, 8, C), F32)
-    for c in range(8):
-        pre[c] = state.reshape(C, C)
-
-        @pl.when(c != chip)
-        def _():
-            back(c).start()
-            remote(tot.at[c], inbox.at[c], fw_send.at[c], fw_recv.at[c], at_chip(c)).wait_recv()
-
-        state = inbox[c, C:MSG, :][None] * state + inbox[c, 0:C, :].reshape(C // 8, 8, C)
-    pin[chip] = pre[chip]
-
-    def hand_over(h):
-        return remote(snd.at[h], st.at[core, h], st_send.at[h], st_recv.at[h], twin)
-
-    def spread(n, carry):
-        h = head_at(n)
-
-        @pl.when(h != chip)
-        def _():
-            remote(pre.at[h], pin.at[h], bk_send.at[h], bk_recv.at[h], at_chip(h)).wait_recv()
-
-        base = pin[h].reshape(C // 8, 8, C)
-        mine_at = loc[core, h, C:MSG, :]
-        sib_at = sib[h, C:MSG, :]
-        mine = mine_at[None] * base + loc[core, h, 0:C, :].reshape(C // 8, 8, C)
-        theirs = sib_at[None] * base + sib[h, 0:C, :].reshape(C // 8, 8, C)
-        first = core == 0
-        snd[h] = jnp.where(first, mine, base).reshape(C, C)
-        st[core, h] = jnp.where(first, base, theirs).reshape(C, C)
-        hand_over(h).start()
-        return carry
-
-    lax.fori_loop(0, H, spread, 0)
+    send_totals(1)
+    spread(0)
 
     def apply(pq, pg, e, w, state, k):
         p = jnp.concatenate([pq, pg], axis=0).astype(BF16)
@@ -380,16 +401,25 @@
         return lax.rem(n, 2) == 0
 
     def turn(i, carry):
+        @pl.when(i == 1)
+        def _():
+            prefix(1)
+
+        @pl.when(i == 3)
+        def _():
+            spread(1)
+
         @pl.when(i < H)
         def _():
             solve(i)
             to_core(i).start()
             out_copy(i).start()
 
-        n1, n2, n3 = i - 1, i - 2, i - 3
+        n1, n2, n3, n4 = i - 1, i - FAR, i - NEAR, i - SAME
         in1 = (i >= 1) & (i < H + 1)
-        in2 = (i >= 2) & (i < H + 2)
-        in3 = (i >= 3) & (i < H + 3)
+        in2 = (i >= FAR) & (i < H + FAR)
+        in3 = (i >= NEAR) & (i < H + NEAR)
+        in4 = (i >= SAME) & (i < H + SAME)
 
         @pl.when(in1)
         def _():
@@ -430,11 +460,11 @@
             far_same(n1).start()
             far_other(n1).start()
 
-        @pl.when(in1 & (core == 1) & odd(n1))
-        def _():
-            far_other(n1 - 1).wait_recv()
-            gp[n1, 1, 2:4, 1 - ylo] = gp[n1, 1, 2:4, 1 - ylo] + zc[n1]
-            send_same(n1).start()
+        @pl.when(in4 & (core == 1) & odd(n4))
+        def _():
+            far_other(n4 - 1).wait_recv()
+            gp[n4, 1, 2:4, 1 - ylo] = gp[n4, 1, 2:4, 1 - ylo] + zc[n4]
+            send_same(n4).start()
 
         @pl.when(in2 & (core == 1) & even(n2))
         def _():
@@ -459,7 +489,7 @@
 
         return carry
 
-    lax.fori_loop(0, H + 3, turn, 0)
+    lax.fori_loop(0, H + NEAR, turn, 0)
 
     acc = None
     own = jnp.where(core == 0, dp * 2 + ylo, xpos * 4 + zpos)
@@ -477,8 +507,9 @@
     def drain(n, carry):
         @pl.when(n != chip)
         def _():
-            forward(n).wait_send()
-            back(n).wait_send()
+            for r in range(2):
+                forward(r, n).wait_send()
+                back(r, n).wait_send()
 
         hand_over(n).wait_send()
         out_copy(n).wait()
@@ -545,10 +576,10 @@
             pltpu.VMEM((H, S, 2 * C, C), F32),
             pltpu.VMEM((2, H, MSG, C), F32),
             pltpu.VMEM((H, MSG, C), F32),
-            pltpu.VMEM((H, MSG, C), F32),
-            pltpu.VMEM((H, MSG, C), F32),
-            pltpu.VMEM((H, C, C), F32),
-            pltpu.VMEM((H, C, C), F32),
+            pltpu.VMEM((2, 8, HALF + 8, C), F32),
+            pltpu.VMEM((2, 8, HALF + 8, C), F32),
+            pltpu.VMEM((2, 8, HALF, C), F32),
+            pltpu.VMEM((2, 8, HALF, C), F32),
             pltpu.VMEM((H, C, C), F32),
             pltpu.VMEM((2, H, C, C), F32),
             pltpu.VMEM((H, 2, 4, 2, C, C), F32),
@@ -561,10 +592,10 @@
             dma((H,)),
             dma((1,)),
             dma((1,)),
-            dma((H,)),
-            dma((H,)),
-            dma((H,)),
-            dma((H,)),
+            dma((2, 8)),
+            dma((2, 8)),
+            dma((2, 8)),
+            dma((2, 8)),
             dma((H,)),
             dma((H,)),
             dma((H,)),
@@ -588,6 +619,44 @@
         regular,
         grad_out.reshape(ROWS, H * C),
     )
+    parts = 4
+    step = ROWS // parts
+
+    def move(a_ref, b_ref, c_ref, d_ref, held, sums, sem_in, sem_out):
+        def a_copy(n):
+            rows = pl.ds(n * step, step)
+            return (
+                pltpu.make_async_copy(a_ref.at[rows], held.at[rows], sem_in.at[n]),
+                pltpu.make_async_copy(held.at[rows], c_ref.at[rows], sem_out.at[n]),
+            )
+
+        pairs = [a_copy(n) for n in range(parts)]
+        pairs.append(
+            (
+                pltpu.make_async_copy(b_ref, sums, sem_in.at[parts]),
+                pltpu.make_async_copy(sums, d_ref, sem_out.at[parts]),
+            )
+        )
+        for come, _ in pairs:
+            come.start()
+        for come, go in pairs:
+            come.wait()
+            go.start()
+        for _, go in pairs:
+            go.wait()
+
+    mixed, query_grad = pl.pallas_call(
+        move,
+        out_shape=(jax.ShapeDtypeStruct(mixed.shape, BF16), jax.ShapeDtypeStruct(query_grad.shape, F32)),
+        in_specs=[hbm, hbm],
+        out_specs=(hbm, hbm),
+        scratch_shapes=[
+            pltpu.VMEM((ROWS, H * C), BF16),
+            pltpu.VMEM((C, C), F32),
+            dma((parts + 1,)),
+            dma((parts + 1,)),
+        ],
+    )(mixed, query_grad)
     return mixed.reshape(1, ROWS, H * C), query_grad
 
 

time: 78.2 us -> 68.3 us (0.87); the launches traced: 77.2 us -> 68.2 us
  Pallas kernels: 72.8 us -> 67.5 us
  local copies, waits for them, and re-layouts: 3.74 us -> 0 us
    pallas_call x1, Pallas kernels: 72.8 us -> 65.5 us  [per_device(): pl.pallas_call(kernel, out_shape=(jax.ShapeDtypeStruct((ROWS, H * C), BF1...]
    unnamed x2 -> x0, local copies, waits for them, and re-layouts: 3.74 us -> none
    pallas_call x0 -> x1, Pallas kernels: none -> 2.01 us  [per_device(): pl.pallas_call(move, out_shape=(jax.ShapeDtypeStruct(mixed.shape, BF16),...]
where the time goes in v3:
time: 68.3 us; the launch traced here: 68.2 us
  Pallas kernels  67.5 us (99%)
    pallas_call x1, Pallas kernels, per_device(): pl.pallas_call(kernel, out_shape=(jax.ShapeDtypeStruct((ROWS, H * C), BF1...  65.5 us
    pallas_call x1, Pallas kernels, per_device(): pl.pallas_call(move, out_shape=(jax.ShapeDtypeStruct(mixed.shape, BF16),...  2.01 us

profile of v3, /device:TPU:1, one launch (start us, length us, event | category | flops | bytes accessed | tf_op | source)
XLA Modules:
  0.0 68.2 jit_solution(7233876901858670308)
XLA Ops:
  0.6 65.5 %shard_map.86 = (bf16[512,1024]{1,0:T(8,128)(2,1)}, f32[128,128]{1,0:T(8,128)}) custom-call(bf16[512,2048]{1,0:T(8,128)(2,1)} %bitcast.6, bf16[2048,1024]{1,0:T(8,128)(2,1)} %wq_hbm.1, bf16[512,1024]{1,0:T(8,128)(2,1)} %bitcast.7, bf16[512,1024]{1,0:T(8,128)(2,1)} %bitcast.8, f32[8,512]{1,0:T(8,128)} %bitcast.10, f32[8]{0:T(128)} %reg_ref.1, ...), custom_call_target="tpu_custom_call" | custom-call | tf_op jit(solution)/shard_map/pallas_call | solution.py:555
  66.1 2.0 %shard_map.87 = (bf16[512,1024]{1,0:T(8,128)(2,1)}, f32[128,128]{1,0:T(8,128)}) custom-call(bf16[512,1024]{1,0:T(8,128)(2,1)} %get-tuple-element.6.a_ref, f32[128,128]{1,0:T(8,128)} %get-tuple-element.7.b_ref), custom_call_target="tpu_custom_call" | custom-call | tf_op jit(solution)/shard_map/pallas_call | solution.py:648

commit v4 on v3

--- a/solution.py
+++ b/solution.py
@@ -75,8 +75,8 @@
             ((k_hbm, kb), (v_hbm, vb), (wq_hbm, wq), (tok_hbm, tok), (g_hbm, gb))
         )
     ]
-    for copy in loads:
-        copy.start()
+    loads[0].start()
+    loads[1].start()
 
     barrier = pltpu.get_barrier_semaphore()
     pl.semaphore_signal(barrier, inc=1, device_id=twin, device_id_type=MESH)
@@ -126,8 +126,11 @@
 
     loads[0].wait()
     loads[1].wait()
-
-    def local_states(h, carry):
+    for copy in (loads[4], loads[3], loads[2]):
+        copy.start()
+
+    def local_states(n, carry):
+        h = head_at(n)
         m_sum = g_sum = None
         decay = None
         for s in range(S):
@@ -152,18 +155,24 @@
                 g_sum = last * g_sum + g_new
                 decay = decay * last
         tile = jnp.broadcast_to(decay, (8, C))
-        loc[0, h, 0:C, :] = m_sum
-        loc[0, h, C:MSG, :] = tile
-        loc[1, h, 0:C, :] = g_sum
-        loc[1, h, C:MSG, :] = tile
+        loc[0, n, 0:C, :] = m_sum
+        loc[0, n, C:MSG, :] = tile
+        loc[1, n, 0:C, :] = g_sum
+        loc[1, n, C:MSG, :] = tile
         return carry
 
-    lax.fori_loop(0, H, local_states, 0)
+    lax.fori_loop(0, 4, local_states, 0)
 
     pl.semaphore_wait(barrier, jnp.where(core == 0, 22, 21))
 
-    to_twin = remote(loc.at[other], sib, sib_send.at[0], sib_recv.at[0], twin)
-    to_twin.start()
+    def to_twin(r):
+        four = pl.ds(4 * r, 4)
+        return remote(loc.at[other, four], sib.at[four], sib_send.at[r], sib_recv.at[r], twin)
+
+    to_twin(0).start()
+
+    lax.fori_loop(4, H, local_states, 0)
+    to_twin(1).start()
 
     loads[4].wait()
 
@@ -183,25 +192,21 @@
             ul[h, s] = (w * dot_nt(gb[rows, lanes(h)], vb[rows, lanes(h)])).astype(BF16)
         return carry
 
-    lax.fori_loop(0, H // 2, tables, 0)
-
-    to_twin.wait_recv()
-
     def unit(r, u):
-        return head_at(4 * r + lax.div(u, 2)), pl.ds(pl.multiple_of(lax.rem(u, 2) * HALF, HALF), HALF)
+        return 4 * r + lax.div(u, 2), pl.ds(pl.multiple_of(lax.rem(u, 2) * HALF, HALF), HALF)
 
     def tiles(block):
         return block.reshape(HALF // 8, 8, C)
 
     def total(r, u):
-        h, half = unit(r, u)
-        mine_at = loc[core, h, C:MSG, :]
-        sib_at = sib[h, C:MSG, :]
+        n, half = unit(r, u)
+        mine_at = loc[core, n, C:MSG, :]
+        sib_at = sib[n, C:MSG, :]
         first = core == 0
         by_mine = jnp.where(first, sib_at, 1.0)
         by_sib = jnp.where(first, 1.0, mine_at)
         tot[r, u, HALF : HALF + 8, :] = mine_at * sib_at
-        mine, theirs = tiles(loc[core, h, half, :]), tiles(sib[h, half, :])
+        mine, theirs = tiles(loc[core, n, half, :]), tiles(sib[n, half, :])
         tot[r, u, 0:HALF, :] = (by_mine[None] * mine + by_sib[None] * theirs).reshape(HALF, C)
 
     def forward(r, u):
@@ -239,9 +244,10 @@
 
     def spread(r):
         def one(e, carry):
-            h = head_at(4 * r + e)
-            mine_at = loc[core, h, C:MSG, :]
-            sib_at = sib[h, C:MSG, :]
+            n = 4 * r + e
+            h = head_at(n)
+            mine_at = loc[core, n, C:MSG, :]
+            sib_at = sib[n, C:MSG, :]
             first = core == 0
             for part in range(2):
                 u = 2 * e + part
@@ -252,8 +258,8 @@
                     remote(pre.at[r, u], pin.at[r, u], bk_send.at[r, u], bk_recv.at[r, u], at_chip(u)).wait_recv()
 
                 base = tiles(pin[r, u])
-                mine = mine_at[None] * base + tiles(loc[core, h, half, :])
-                theirs = sib_at[None] * base + tiles(sib[h, half, :])
+                mine = mine_at[None] * base + tiles(loc[core, n, half, :])
+                theirs = sib_at[None] * base + tiles(sib[n, half, :])
                 snd[h, half, :] = jnp.where(first, mine, base).reshape(HALF, C)
                 st[core, h, half, :] = jnp.where(first, base, theirs).reshape(HALF, C)
             hand_over(h).start()
@@ -261,9 +267,10 @@
 
         lax.fori_loop(0, 4, one, 0)
 
+    to_twin(0).wait_recv()
     send_totals(0)
 
-    lax.fori_loop(H // 2, H, tables, 0)
+    lax.fori_loop(0, H, tables, 0)
 
     prefix(0)
 
@@ -274,6 +281,7 @@
         qb[2 * n] = block[:, 0:C]
         qb[2 * n + 1] = block[:, C : 2 * C]
 
+    to_twin(1).wait_recv()
     send_totals(1)
     spread(0)
 
@@ -502,7 +510,8 @@
         acc = fin[source] if acc is None else acc + fin[source]
     qg_ref[...] = acc
 
-    to_twin.wait_send()
+    to_twin(0).wait_send()
+    to_twin(1).wait_send()
 
     def drain(n, carry):
         @pl.when(n != chip)
@@ -590,8 +599,8 @@
             pltpu.VMEM((16, C, C), F32),
             dma((5,)),
             dma((H,)),
-            dma((1,)),
-            dma((1,)),
+            dma((2,)),
+            dma((2,)),
             dma((2, 8)),
             dma((2, 8)),
             dma((2, 8)),

time: 68.3 us -> 67.2 us (0.984)
  Pallas kernels: 67.5 us -> 66.3 us
    pallas_call x1, Pallas kernels: 65.5 us -> 64.3 us  [per_device(): pl.pallas_call(kernel, out_shape=(jax.ShapeDtypeStruct((ROWS, H * C), BF1...]
where the time goes in v4:
time: 67.2 us; the launch traced here: 67 us
  Pallas kernels  66.3 us (99%)
    pallas_call x1, Pallas kernels, per_device(): pl.pallas_call(kernel, out_shape=(jax.ShapeDtypeStruct((ROWS, H * C), BF1...  64.3 us
    pallas_call x1, Pallas kernels, per_device(): pl.pallas_call(move, out_shape=(jax.ShapeDtypeStruct(mixed.shape, BF16),...  2.01 us

profile of v4, /device:TPU:1, one launch (start us, length us, event | category | flops | bytes accessed | tf_op | source)
XLA Modules:
  0.0 67.0 jit_solution(16034484879105402935)
XLA Ops:
  0.6 64.3 %shard_map.86 = (bf16[512,1024]{1,0:T(8,128)(2,1)}, f32[128,128]{1,0:T(8,128)}) custom-call(bf16[512,2048]{1,0:T(8,128)(2,1)} %bitcast.6, bf16[2048,1024]{1,0:T(8,128)(2,1)} %wq_hbm.1, bf16[512,1024]{1,0:T(8,128)(2,1)} %bitcast.7, bf16[512,1024]{1,0:T(8,128)(2,1)} %bitcast.8, f32[8,512]{1,0:T(8,128)} %bitcast.10, f32[8]{0:T(128)} %reg_ref.1, ...), custom_call_target="tpu_custom_call" | custom-call | tf_op jit(solution)/shard_map/pallas_call | solution.py:564
  65.0 2.0 %shard_map.87 = (bf16[512,1024]{1,0:T(8,128)(2,1)}, f32[128,128]{1,0:T(8,128)}) custom-call(bf16[512,1024]{1,0:T(8,128)(2,1)} %get-tuple-element.6.a_ref, f32[128,128]{1,0:T(8,128)} %get-tuple-element.7.b_ref), custom_call_target="tpu_custom_call" | custom-call | tf_op jit(solution)/shard_map/pallas_call | solution.py:657

commit v5 on v4

--- a/solution.py
+++ b/solution.py
@@ -277,12 +277,13 @@
     loads[2].wait()
     loads[3].wait()
     for n in range(H // 2):
+        if n == 2:
+            to_twin(1).wait_recv()
+            send_totals(1)
         block = dot(tok[...], wq[:, n * 2 * C : (n + 1) * 2 * C]).astype(BF16)
         qb[2 * n] = block[:, 0:C]
         qb[2 * n + 1] = block[:, C : 2 * C]
 
-    to_twin(1).wait_recv()
-    send_totals(1)
     spread(0)
 
     def apply(pq, pg, e, w, state, k):

time: 67.2 us -> 67.2 us (level)
  no operation moved by 1% of the time
where the time goes in v5:
time: 67.2 us; the launch traced here: 67 us
  Pallas kernels  66.3 us (99%)
    pallas_call x1, Pallas kernels, per_device(): pl.pallas_call(kernel, out_shape=(jax.ShapeDtypeStruct((ROWS, H * C), BF1...  64.3 us
    pallas_call x1, Pallas kernels, per_device(): pl.pallas_call(move, out_shape=(jax.ShapeDtypeStruct(mixed.shape, BF16),...  2.01 us

profile of v5, /device:TPU:1, one launch (start us, length us, event | category | flops | bytes accessed | tf_op | source)
XLA Modules:
  0.0 67.0 jit_solution(8967860449512232761)
XLA Ops:
  0.6 64.3 %shard_map.86 = (bf16[512,1024]{1,0:T(8,128)(2,1)}, f32[128,128]{1,0:T(8,128)}) custom-call(bf16[512,2048]{1,0:T(8,128)(2,1)} %bitcast.6, bf16[2048,1024]{1,0:T(8,128)(2,1)} %wq_hbm.1, bf16[512,1024]{1,0:T(8,128)(2,1)} %bitcast.7, bf16[512,1024]{1,0:T(8,128)(2,1)} %bitcast.8, f32[8,512]{1,0:T(8,128)} %bitcast.10, f32[8]{0:T(128)} %reg_ref.1, ...), custom_call_target="tpu_custom_call" | custom-call | tf_op jit(solution)/shard_map/pallas_call | solution.py:565
  65.0 2.0 %shard_map.87 = (bf16[512,1024]{1,0:T(8,128)(2,1)}, f32[128,128]{1,0:T(8,128)}) custom-call(bf16[512,1024]{1,0:T(8,128)(2,1)} %get-tuple-element.6.a_ref, f32[128,128]{1,0:T(8,128)} %get-tuple-element.7.b_ref), custom_call_target="tpu_custom_call" | custom-call | tf_op jit(solution)/shard_map/pallas_call | solution.py:658

commit v6 on v5

--- a/solution.py
+++ b/solution.py
@@ -277,7 +277,7 @@
     loads[2].wait()
     loads[3].wait()
     for n in range(H // 2):
-        if n == 2:
+        if n == 1:
             to_twin(1).wait_recv()
             send_totals(1)
         block = dot(tok[...], wq[:, n * 2 * C : (n + 1) * 2 * C]).astype(BF16)

time: 67.2 us -> 67.2 us (level)
  no operation moved by 1% of the time
where the time goes in v6:
time: 67.2 us; the launch traced here: 67 us
  Pallas kernels  66.3 us (99%)
    pallas_call x1, Pallas kernels, per_device(): pl.pallas_call(kernel, out_shape=(jax.ShapeDtypeStruct((ROWS, H * C), BF1...  64.3 us
    pallas_call x1, Pallas kernels, per_device(): pl.pallas_call(move, out_shape=(jax.ShapeDtypeStruct(mixed.shape, BF16),...  2.01 us

profile of v6, /device:TPU:1, one launch (start us, length us, event | category | flops | bytes accessed | tf_op | source)
XLA Modules:
  0.0 67.0 jit_solution(828821379366873826)
XLA Ops:
  0.6 64.3 %shard_map.86 = (bf16[512,1024]{1,0:T(8,128)(2,1)}, f32[128,128]{1,0:T(8,128)}) custom-call(bf16[512,2048]{1,0:T(8,128)(2,1)} %bitcast.6, bf16[2048,1024]{1,0:T(8,128)(2,1)} %wq_hbm.1, bf16[512,1024]{1,0:T(8,128)(2,1)} %bitcast.7, bf16[512,1024]{1,0:T(8,128)(2,1)} %bitcast.8, f32[8,512]{1,0:T(8,128)} %bitcast.10, f32[8]{0:T(128)} %reg_ref.1, ...), custom_call_target="tpu_custom_call" | custom-call | tf_op jit(solution)/shard_map/pallas_call | solution.py:565
  65.0 2.0 %shard_map.87 = (bf16[512,1024]{1,0:T(8,128)(2,1)}, f32[128,128]{1,0:T(8,128)}) custom-call(bf16[512,1024]{1,0:T(8,128)(2,1)} %get-tuple-element.6.a_ref, f32[128,128]{1,0:T(8,128)} %get-tuple-element.7.b_ref), custom_call_target="tpu_custom_call" | custom-call | tf_op jit(solution)/shard_map/pallas_call | solution.py:658
